TPU v7x, 256 devices: a whole 4x4x8 slice. The times are simulated.
256 devices in a mesh: depth: 2 (over core), row: 16 (over y, x), col: 8 (over z).
Axes of the slice: x: 4, y: 4, z: 8, core: 2. Of those that a mesh axis runs over, the one named last changes fastest.
Arguments:
- inputs: bfloat16 [256, 12288], P(('depth', 'col'), 'row'), may hold values from -6 to 6
- up_blocks: bfloat16 [16, 8, 108, 128, 128], P('row', 'col'), may hold values from -0.109375 to 0.109375
- down_blocks: bfloat16 [16, 8, 108, 128, 128], P('row', 'col'), may hold values from -0.0546875 to 0.0546875
- slots: int32 [16, 8, 108], P('row', 'col'), may hold values from 0 to 287, as said below
- counts: int32 [16, 8], P('row', 'col'), may hold values from 27 to 108, as said below
- grad_out: bfloat16 [256, 12288], P(('depth', 'col'), 'row'), may hold values from -6 to 6
Outputs:
- outputs: bfloat16 [256, 12288], P(('depth', 'col'), 'row')
- grad_in: bfloat16 [256, 12288], P(('depth', 'col'), 'row')
- grad_up: bfloat16 [16, 8, 108, 128, 128], P('row', 'col', 'depth')
- grad_down: bfloat16 [16, 8, 108, 128, 128], P('row', 'col', 'depth')
Inputs may be any that keep to these rules, and one draw needn't show every extreme that they name: `slots`: within each tile the 108 slot numbers are distinct local block numbers of 0 to 287. `counts`: some tile is full and some tile has the fewest live slots.
All inputs are finite; a program needn't handle non-finite values.
Results may differ from a plain program's by a relative error of at most 0.0059.
Values may be sent and summed in bfloat16 or wider, within the bound.
A program may use at most 128 MiB of HBM per device.

v0:
```python
import jax
import jax.numpy as jnp
from jax import lax
from jax.sharding import PartitionSpec as P

FF = 49152


root_coeff = 0.7978845608
cube_coeff = 0.044715


def gelu_parts(preact):
    cubed = preact * preact * preact
    tangent = jnp.tanh(root_coeff * (preact + cube_coeff * cubed))
    values = 0.5 * preact * (1.0 + tangent)
    slopes = 0.5 * (1.0 + tangent) + 0.5 * preact * (1.0 - tangent * tangent) * root_coeff * (
        1.0 + 3.0 * cube_coeff * preact * preact
    )
    return (values, slopes)


def pick_blocks(rows_in, block_ids, block_size):
    height = rows_in.shape[0]
    return rows_in.reshape(height, -1, block_size)[:, block_ids, :]


def spread_blocks(products, block_ids, block_count):
    height, slot_count, block_size = products.shape
    placing = (block_ids[:, None] == jnp.arange(block_count)[None, :]).astype(jnp.float32)
    summed = jnp.einsum("tsb,sf->tfb", products, placing, precision=lax.Precision.HIGHEST)
    return summed.reshape(height, block_count * block_size)


def on_device(inputs, up_blocks, down_blocks, slots, counts, grad_out):
    block_size = up_blocks.shape[-1]
    capacity = up_blocks.shape[2]
    width_blocks = inputs.shape[1] // block_size
    hidden_blocks = FF // lax.axis_size("col") // block_size
    slot_ids = slots[0, 0]
    block_in = slot_ids // hidden_blocks
    block_out = slot_ids % hidden_blocks
    alive_count = counts[0, 0]
    alive_mask = (jnp.arange(capacity) < alive_count).astype(jnp.float32)
    alive_half = alive_mask.astype(jnp.bfloat16)
    weight_one = up_blocks[0, 0] * alive_half[:, None, None]
    weight_two = down_blocks[0, 0] * alive_half[:, None, None]
    tok_rows, grad_rows = (
        lax.all_gather(inputs, "col", axis=0, tiled=True),
        lax.all_gather(grad_out, "col", axis=0, tiled=True),
    )
    sliced = tok_rows
    chosen = pick_blocks(sliced, block_in, block_size)
    preact = lax.psum_scatter(
        spread_blocks(
            jnp.einsum("tsa,sab->tsb", chosen, weight_one, preferred_element_type=jnp.float32),
            block_out,
            hidden_blocks,
        ),
        "row",
        scatter_dimension=0,
        tiled=True,
    )
    values, slopes = gelu_parts(preact)
    hidden_share = values.astype(jnp.bfloat16)
    hidden = lax.all_gather(hidden_share, "row", axis=0, tiled=True)
    sliced = grad_rows
    chosen = pick_blocks(sliced, block_in, block_size)
    grad_hidden = lax.psum_scatter(
        spread_blocks(
            jnp.einsum("tsa,sba->tsb", chosen, weight_two, preferred_element_type=jnp.float32),
            block_out,
            hidden_blocks,
        ),
        "row",
        scatter_dimension=0,
        tiled=True,
    )
    grad_pre_share = (grad_hidden * slopes).astype(jnp.bfloat16)
    grad_pre = lax.all_gather(grad_pre_share, "row", axis=0, tiled=True)
    sliced = hidden
    chosen = pick_blocks(sliced, block_out, block_size)
    outputs = lax.psum_scatter(
        spread_blocks(
            jnp.einsum("tsb,sba->tsa", chosen, weight_two, preferred_element_type=jnp.float32),
            block_in,
            width_blocks,
        ),
        "col",
        scatter_dimension=0,
        tiled=True,
    ).astype(jnp.bfloat16)
    sliced = grad_pre
    chosen = pick_blocks(sliced, block_out, block_size)
    grad_in = lax.psum_scatter(
        spread_blocks(
            jnp.einsum("tsb,sab->tsa", chosen, weight_one, preferred_element_type=jnp.float32),
            block_in,
            width_blocks,
        ),
        "col",
        scatter_dimension=0,
        tiled=True,
    ).astype(jnp.bfloat16)
    tok_picked = pick_blocks(tok_rows, block_in, block_size)
    grad_picked = pick_blocks(grad_rows, block_in, block_size)
    hidden_picked = pick_blocks(hidden, block_out, block_size)
    pre_picked = pick_blocks(grad_pre, block_out, block_size)
    part_up = (
        jnp.einsum("tsa,tsb->sab", tok_picked, pre_picked, preferred_element_type=jnp.float32)
        * alive_mask[:, None, None]
    )
    part_down = (
        jnp.einsum("tsb,tsa->sba", hidden_picked, grad_picked, preferred_element_type=jnp.float32)
        * alive_mask[:, None, None]
    )
    summed_up, summed_down = (
        lax.psum_scatter(
            part_up.astype(jnp.bfloat16), "depth", scatter_dimension=0, tiled=True
        ).astype(jnp.float32),
        lax.psum_scatter(
            part_down.astype(jnp.bfloat16), "depth", scatter_dimension=0, tiled=True
        ).astype(jnp.float32),
    )
    grad_up = summed_up.astype(jnp.bfloat16)[None, None]
    grad_down = summed_down.astype(jnp.bfloat16)[None, None]
    return (outputs, grad_in, grad_up, grad_down)


def solution(mesh):
    return jax.shard_map(
        on_device,
        mesh=mesh,
        in_specs=(
            P(("depth", "col"), "row"),
            P("row", "col", None, None, None),
            P("row", "col", None, None, None),
            P("row", "col", None),
            P("row", "col"),
            P(("depth", "col"), "row"),
        ),
        out_specs=(
            P(("depth", "col"), "row"),
            P(("depth", "col"), "row"),
            P("row", "col", "depth", None, None),
            P("row", "col", "depth", None, None),
        ),
        check_vma=False,
    )
```

profile of v0, /device:TPU:1, one launch (start us, length us, event | category | flops | bytes accessed | tf_op | source)
XLA Modules:
  0.0 518.3 jit_solution(8874160698147855267)
XLA Ops:
  8.6 23.4 %all_gather.14 = bf16[128,768]{1,0:T(8,128)(2,1)S(1)} all-gather(bf16[16,768]{1,0:T(8,128)(2,1)} %param.11), channel_id=1, replica_groups=mesh['depth'=2,'row'=16,'col'=8] {'col'}, dimensions={0}, use_global_device_ids=true | all-gather | bytes 221184 | tf_op jit(solution)/shard_map/all_gather | solution.py:50
  32.9 2.8 gather_fusion.2
  35.8 8.6 %fusion.20 = f32[128,108,128]{0,2,1:T(8,128)} fusion(bf16[108,128,128]{2,1,0:T(8,128)(2,1)} %gather_fusion.2, bf16[1,1,108,128,128]{4,3,2,1,0:T(8,128)(2,1)} %param.8, bf16[108]{0:T(256)(128)(2,1)S(1)} %get-tuple-element.32), kind=kOutput, calls=%fused_computation.24 | convolution fusion | flops 454754304 | bytes 14155992 | tf_op jit(solution)/shard_map/tsa,sba->tsb/dot_general | solution.py:71
  44.4 8.1 %copy.82 = f32[128,108,128]{2,1,0:T(8,128)} copy(f32[128,108,128]{0,2,1:T(8,128)} %fusion.20) | data formatting | bytes 14155776 | tf_op jit(solution)/shard_map/tsa,sba->tsb/transpose | solution.py:71
  52.5 5.0 convolution_bitcast_fusion
  57.6 2.3 copy.100
  59.9 18.3 %all_gather.12 = bf16[128,768]{1,0:T(8,128)(2,1)S(1)} all-gather(bf16[16,768]{1,0:T(8,128)(2,1)S(1)} %copy-done.3), channel_id=1, replica_groups=mesh['depth'=2,'row'=16,'col'=8] {'col'}, dimensions={0}, use_global_device_ids=true | all-gather | bytes 221184 | tf_op jit(solution)/shard_map/all_gather | solution.py:49
  78.6 2.8 gather_fusion
  81.4 8.7 %fusion.14 = f32[128,108,128]{0,2,1:T(8,128)} fusion(bf16[108,128,128]{2,1,0:T(8,128)(2,1)} %gather_fusion, bf16[1,1,108,128,128]{4,3,2,1,0:T(8,128)(2,1)} %param.7, bf16[108]{0:T(256)(128)(2,1)S(1)} %get-tuple-element.32), kind=kOutput, calls=%fused_computation.22 | convolution fusion | flops 454754304 | bytes 14155992 | tf_op jit(solution)/shard_map/tsa,sab->tsb/dot_general | solution.py:56
  90.1 8.1 %copy.68 = f32[128,108,128]{2,1,0:T(8,128)} copy(f32[128,108,128]{0,2,1:T(8,128)} %fusion.14) | data formatting | bytes 14155776 | tf_op jit(solution)/shard_map/tsa,sab->tsb/transpose | solution.py:56
  98.3 5.0 convolution_bitcast_fusion.1
  103.3 2.4 copy.99
  107.6 142.6 %all-reduce.5.cloned.1.call-done = (f32[128,6144]{0,1:T(8,128)}, f32[128,6144]{0,1:T(8,128)}) async-done(((f32[128,6144]{0,1:T(8,128)}, f32[128,6144]{0,1:T(8,128)}), (f32[128,6144]{0,1:T(8,128)}, f32[128,6144]{0,1:T(8,128)})) %all-reduce.5.cloned.1.call-update) | async-done | bytes 6291472
  250.2 2.8 constant_dynamic-slice_fusion.1
  254.1 2.8 constant_dynamic-slice_fusion
  259.6 47.2 %all-gather.5.cloned.1.call-done = bf16[128,6144]{1,0:T(8,128)(2,1)} async-done(((bf16[8,6144]{1,0:T(8,128)(2,1)}), bf16[128,6144]{1,0:T(8,128)(2,1)}) %all-gather.5.cloned.1.call-update) | async-done | bytes 1572880 | tf_op jit(solution)/shard_map/all_gather | solution.py:80
  309.6 48.9 %all-gather.3.cloned.1.call-done = bf16[128,6144]{1,0:T(8,128)(2,1)} async-done(((bf16[8,6144]{1,0:T(8,128)(2,1)}), bf16[128,6144]{1,0:T(8,128)(2,1)}) %all-gather.3.cloned.1.call-update) | async-done | bytes 1572880 | tf_op jit(solution)/shard_map/all_gather | solution.py:66
  362.0 2.9 gather_fusion.3
  364.8 2.6 gather_fusion.1
  367.5 9.9 %fusion.23 = f32[128,108,128]{0,2,1:T(8,128)} fusion(bf16[108,128,128]{2,1,0:T(8,128)(2,1)} %gather_fusion.3, bf16[1,1,108,128,128]{4,3,2,1,0:T(8,128)(2,1)} %param.7, bf16[108]{0:T(256)(128)(2,1)S(1)} %get-tuple-element.32), kind=kOutput, calls=%fused_computation.25 | convolution fusion | flops 454754304 | bytes 14155992 | tf_op jit(solution)/shard_map/tsb,sab->tsa/dot_general | solution.py:97
  377.4 8.1 %copy.89 = f32[128,108,128]{2,1,0:T(8,128)} copy(f32[128,108,128]{0,2,1:T(8,128)} %fusion.23) | data formatting | bytes 14155776 | tf_op jit(solution)/shard_map/tsb,sab->tsa/transpose | solution.py:97
  385.5 6.3 %convolution_bitcast_fusion.2 = f32[128,6,128]{2,1,0:T(8,128)} fusion(f32[128,108,128]{2,1,0:T(8,128)} %copy.89, s32[108]{0:T(128)S(1)} %get-tuple-element.22), kind=kOutput, calls=%fused_computation.32 | convolution fusion | flops 127402632 | bytes 7471536 | tf_op jit(solution)/shard_map/tsb,sf->tfb/dot_general | solution.py:31
  391.9 2.0 copy.90
  396.0 7.6 %fusion.17 = f32[128,108,128]{0,2,1:T(8,128)} fusion(bf16[108,128,128]{2,1,0:T(8,128)(2,1)S(1)} %gather_fusion.1, bf16[1,1,108,128,128]{4,3,2,1,0:T(8,128)(2,1)} %param.8, bf16[108]{0:T(256)(128)(2,1)S(1)} %get-tuple-element.32), kind=kOutput, calls=%fused_computation.23 | convolution fusion | flops 454754304 | bytes 14155992 | tf_op jit(solution)/shard_map/tsb,sba->tsa/dot_general | solution.py:85
  403.7 8.1 %copy.78 = f32[128,108,128]{2,1,0:T(8,128)} copy(f32[128,108,128]{0,2,1:T(8,128)} %fusion.17) | data formatting | bytes 14155776 | tf_op jit(solution)/shard_map/tsb,sba->tsa/transpose | solution.py:85
  411.8 6.5 %convolution_bitcast_fusion.3 = f32[128,6,128]{2,1,0:T(8,128)} fusion(f32[128,108,128]{2,1,0:T(8,128)} %copy.78, s32[108]{0:T(128)S(1)} %get-tuple-element.22), kind=kOutput, calls=%fused_computation.33 | convolution fusion | flops 127402632 | bytes 7471536 | tf_op jit(solution)/shard_map/tsb,sf->tfb/dot_general | solution.py:31
  418.3 2.0 copy.79
  422.3 5.6 %multiply_convert_fusion.1 = bf16[108,128,128]{2,1,0:T(8,128)(2,1)} fusion(f32[108]{0:T(128)S(1)} %get-tuple-element.31, bf16[108,128,128]{2,1,0:T(8,128)(2,1)} %gather_fusion.3, bf16[108,128,128]{2,1,0:T(8,128)(2,1)S(1)} %copy-done.1), kind=kOutput, calls=%fused_computation.5 | convolution fusion | flops 456523776 | bytes 10617264 | tf_op jit(solution)/shard_map/tsa,tsb->sab/dot_general | solution.py:110
  429.8 5.5 %multiply_convert_fusion = bf16[108,128,128]{2,1,0:T(8,128)(2,1)} fusion(f32[108]{0:T(128)S(1)} %get-tuple-element.31, bf16[108,128,128]{2,1,0:T(8,128)(2,1)S(1)} %copy-done, bf16[108,128,128]{2,1,0:T(8,128)(2,1)} %copy-done.2), kind=kOutput, calls=%fused_computation.4 | convolution fusion | flops 456523776 | bytes 10617264 | tf_op jit(solution)/shard_map/tsb,tsa->sba/dot_general | solution.py:114
  437.1 29.4 %reduce-scatter.15.cloned.1.call-done = f32[16,768]{1,0:T(8,128)} async-done(((f32[128,768]{1,0:T(8,128)}), f32[16,768]{1,0:T(8,128)}) %reduce-scatter.15.cloned.1.call-update) | async-done | bytes 49168
  468.3 22.1 %reduce-scatter.11.cloned.1.call-done = bf16[54,128,128]{2,1,0:T(8,128)(2,1)} async-done(((bf16[108,128,128]{2,1,0:T(8,128)(2,1)}), bf16[54,128,128]{2,1,0:T(8,128)(2,1)}) %reduce-scatter.11.cloned.1.call-update) | async-done | bytes 1769488 | tf_op jit(solution)/shard_map/reduce_scatter | solution.py:118
  490.3 21.1 %reduce-scatter.13.cloned.1.call-done = bf16[54,128,128]{2,1,0:T(8,128)(2,1)} async-done(((bf16[108,128,128]{2,1,0:T(8,128)(2,1)}), bf16[54,128,128]{2,1,0:T(8,128)(2,1)}) %reduce-scatter.13.cloned.1.call-update) | async-done | bytes 1769488 | tf_op jit(solution)/shard_map/reduce_scatter | solution.py:121
  (47 shorter events, 23.0 us)
Async XLA Ops:
  7.2 243.1 %all-reduce.5.cloned.1.call-start = ((), (), s32[]{:S(2)}) async-start(), calls=%async_computation.10 | async-start | bytes 12582912
  57.6 2.4 copy-start.3
  105.7 0.7 copy-start.4
  105.7 201.0 %all-gather.5.cloned.1.call-start = ((), (), s32[]{:S(2)}) async-start(), calls=%async_computation.5 | async-start | bytes 1671168 | tf_op jit(solution)/shard_map/all_gather | solution.py:80
  258.8 99.7 %all-gather.3.cloned.1.call-start = ((), (), s32[]{:S(2)}) async-start(), calls=%async_computation.4 | async-start | bytes 1671168 | tf_op jit(solution)/shard_map/all_gather | solution.py:66
  259.5 175.9 %reduce-scatter.17.cloned.1.call-start = ((), (), s32[]{:S(2)}) async-start(), calls=%async_computation.9 | async-start | bytes 442368
  367.5 28.5 %copy-start.2 = (bf16[108,128,128]{2,1,0:T(8,128)(2,1)}, bf16[108,128,128]{2,1,0:T(8,128)(2,1)S(1)}, u32[]{:S(2)}) copy-start(bf16[108,128,128]{2,1,0:T(8,128)(2,1)S(1)} %gather_fusion.1) | copy-start | bytes 10616836
  395.7 70.8 %reduce-scatter.15.cloned.1.call-start = ((), (), s32[]{:S(2)}) async-start(), calls=%async_computation.8 | async-start | bytes 442368
  411.8 10.5 %copy-start.1 = (bf16[108,128,128]{2,1,0:T(8,128)(2,1)S(1)}, bf16[108,128,128]{2,1,0:T(8,128)(2,1)}, u32[]{:S(2)}) copy-start(bf16[108,128,128]{2,1,0:T(8,128)(2,1)} %gather_fusion) | copy-start | bytes 10616836
  422.2 68.1 %reduce-scatter.11.cloned.1.call-start = ((), (), s32[]{:S(2)}) async-start(), calls=%async_computation.6 | async-start | bytes 5308416 | tf_op jit(solution)/shard_map/reduce_scatter | solution.py:118
  427.8 2.0 copy-start
  427.9 83.6 %reduce-scatter.13.cloned.1.call-start = ((), (), s32[]{:S(2)}) async-start(), calls=%async_computation.7 | async-start | bytes 5308416 | tf_op jit(solution)/shard_map/reduce_scatter | solution.py:121
Sparse Core Ops, SparseCore 0:
  105.9 144.3 all-reduce.4
  258.9 47.8 all-gather.4
  310.1 48.3 all-gather.2
  395.9 32.6 reduce-scatter.16
  430.9 35.6 reduce-scatter.14
  469.6 20.6 reduce-scatter.10
  493.4 17.9 reduce-scatter.12
where the time goes:
time: 519 us; the launch traced here: 518 us
  waiting for transfers between devices  312 us (60%)
  local copies, waits for them, and re-layouts  77.2 us (15%)
  matrix products  68.9 us (13%)
  blocking collectives  41.7 us (8%)
  between operations  15.6 us (3%)
    unnamed x10, waiting for transfers between devices  173 us
    all_gather x1, waiting for transfers between devices, on_device(): hidden = lax.all_gather(hidden_share, 'row', axis=0, tiled=True)  48.9 us
    all_gather x1, waiting for transfers between devices, on_device(): grad_pre = lax.all_gather(grad_pre_share, 'row', axis=0, tiled=True)  47.2 us
    all_gather x1, blocking collectives, on_device(): lax.all_gather(grad_out, 'col', axis=0, tiled=True)  23.4 us
    dot_general x4, matrix products, spread_blocks(): jnp.einsum('tsb,sf->tfb', products, placing, precision=lax.Precision.HIGH...  22.9 us
    reduce_scatter x1, waiting for transfers between devices, on_device(): lax.psum_scatter(part_up.astype(jnp.bfloat16), 'depth', scatter_dimension...  22.1 us
    reduce_scatter x1, waiting for transfers between devices, on_device(): lax.psum_scatter(part_down.astype(jnp.bfloat16), 'depth', scatter_dimensi...  21.1 us
    all_gather x1, blocking collectives, on_device(): lax.all_gather(inputs, 'col', axis=0, tiled=True)  18.3 us
  transfers between devices with their start and end apart: 7, of which 6 were waited for; matrix products, arithmetic and copies ran while one was open for 8% of the time, Pallas kernels for 0%

commit v1 on v0

v1 whole, which is shorter than its diff:
```python
import jax
import jax.numpy as jnp
from jax import lax
from jax.experimental import pallas as pl
from jax.experimental.pallas import tpu as pltpu
from jax.sharding import PartitionSpec as P

MESH = pl.DeviceIdType.MESH
F32, BF16 = jnp.float32, jnp.bfloat16
BLK, CAP, HALF = 128, 108, 54
WB, FB = 6, 48
NX, NY, NZ = 4, 4, 8
CHUNKS = 3
ROWS = 16

root_coeff = 0.7978845608
cube_coeff = 0.044715


def gelu_parts(preact):
    cubed = preact * preact * preact
    tangent = jnp.tanh(root_coeff * (preact + cube_coeff * cubed))
    values = 0.5 * preact * (1.0 + tangent)
    slopes = 0.5 * (1.0 + tangent) + 0.5 * preact * (1.0 - tangent * tangent) * root_coeff * (
        1.0 + 3.0 * cube_coeff * preact * preact
    )
    return (values, slopes)


def dot(a, b):
    return lax.dot_general(a, b, (((1,), (0,)), ((), ())), preferred_element_type=F32)


def dot_t(a, b):
    return lax.dot_general(a, b, (((1,), (1,)), ((), ())), preferred_element_type=F32)


def quad(a, b, c, d):
    return jnp.concatenate(
        [jnp.concatenate([a, b], axis=1), jnp.concatenate([c, d], axis=1)], axis=0
    )


def kernel(
    inv, slots, counts, x_in, g_in, up_in, dn_in,
    out_ref, gin_ref, gup_ref, gdn_ref,
    up, dn, xs, gs, xt, gt, pbuf, gbuf, r1p, r1g, s2p, s2g, ownp, owng, r2p, r2g,
    hid, pre, acc_o, acc_i, send_o, send_i, recv_o, recv_i, gup_v, gdn_v,
    wsem, lsem, ssem_a, rsem_a, ssem_1, rsem_1, ssem_2, rsem_2, ssem_h, rsem_h, ssem_q, rsem_q,
    ssem_d, rsem_d, ssem_z, rsem_z, osem,
):
    d, r, c = lax.axis_index("depth"), lax.axis_index("row"), lax.axis_index("col")
    y, x = r // NX, r % NX
    sends = []

    def at_x(o):
        return (d, y * NX + (x + o) % NX, c)

    def at_y(o):
        return (d, ((y + o) % NY) * NX + x, c)

    def at_z(o):
        return (d, r, (c + o) % NZ)

    partner = (1 - d, r, c)

    def remote(src, dst, ssem, rsem, device):
        copy = pltpu.make_async_remote_copy(
            src_ref=src, dst_ref=dst, send_sem=ssem, recv_sem=rsem, device_id=device, device_id_type=MESH
        )
        copy.start()
        sends.append(copy)
        return copy

    load_up = pltpu.make_async_copy(up_in.at[0, 0], up.at[pl.ds(0, CAP)], wsem.at[0])
    load_dn = pltpu.make_async_copy(dn_in.at[0, 0], dn.at[pl.ds(0, CAP)], wsem.at[1])
    mine = pl.ds(pl.multiple_of(c * ROWS, ROWS), ROWS)
    load_x = pltpu.make_async_copy(x_in, xs.at[0, mine], lsem.at[0])
    load_g = pltpu.make_async_copy(g_in, gs.at[0, mine], lsem.at[1])
    load_x.start()
    load_g.start()
    load_up.start()
    load_dn.start()
    up[CAP] = jnp.zeros((BLK, BLK), BF16)
    dn[CAP] = jnp.zeros((BLK, BLK), BF16)

    barrier = pltpu.get_barrier_semaphore()
    peers = [at_x(o) for o in (1, 2, 3)] + [at_y(o) for o in (1, 2, 3)]
    peers += [at_z(o) for o in range(1, NZ)] + [partner]
    for peer in peers:
        pl.semaphore_signal(barrier, inc=1, device_id=peer, device_id_type=MESH)
    pl.semaphore_wait(barrier, len(peers))

    far_first = (4, 3, 5, 2, 6, 1, 7)
    got_x, got_g = [], []
    for n, (src, dst, got) in enumerate(((x_in, xs, got_x), (g_in, gs, got_g))):
        for o in far_first:
            got.append(remote(src, dst.at[0, mine], ssem_a.at[n, o - 1], rsem_a.at[n, o - 1], at_z(o)))

    def block(weights, i, f):
        return weights[inv[i * FB + f]]

    def pair_p(fa, fb):
        acc = None
        for kk in range(3):
            w = quad(block(up, 2 * kk, fa), block(up, 2 * kk, fb), block(up, 2 * kk + 1, fa), block(up, 2 * kk + 1, fb))
            term = dot(xs[0, :, 256 * kk : 256 * kk + 256], w)
            acc = term if acc is None else acc + term
        return acc

    def pair_g(fa, fb):
        acc = None
        for kk in range(3):
            w = quad(block(dn, 2 * kk, fa), block(dn, 2 * kk + 1, fa), block(dn, 2 * kk, fb), block(dn, 2 * kk + 1, fb))
            term = dot_t(gs[0, :, 256 * kk : 256 * kk + 256], w)
            acc = term if acc is None else acc + term
        return acc

    got_1p, got_1g, got_2p, got_2g = {}, {}, {}, {}

    def make_p(k):
        for o in (2, 1, 3, 0):
            xx = (x + o) % NX

            def body(m, carry, xx=xx):
                fa = 16 * k + 8 * m + xx
                acc = pair_p(fa, fa + NX).astype(BF16)
                pbuf[k, xx * 4 + 2 * m] = acc[:, :BLK]
                pbuf[k, xx * 4 + 2 * m + 1] = acc[:, BLK:]
                return carry

            lax.fori_loop(0, 2, body, 0)
            if o:
                got_1p[k, o] = remote(
                    pbuf.at[k, pl.ds(xx * 4, 4)], r1p.at[k, o - 1], ssem_1.at[0, k, o - 1], rsem_1.at[0, k, o - 1], at_x(o)
                )

    def make_g(k):
        for o in (2, 1, 3, 0):
            yy = (y + o) % NY

            def body(m, carry, yy=yy):
                fa = 16 * k + 4 * yy + 2 * m
                acc = pair_g(fa, fa + 1).astype(BF16)
                gbuf[k, yy * 4 + 2 * m] = acc[:, :BLK]
                gbuf[k, yy * 4 + 2 * m + 1] = acc[:, BLK:]
                return carry

            lax.fori_loop(0, 2, body, 0)
            if o:
                got_1g[k, o] = remote(
                    gbuf.at[k, pl.ds(yy * 4, 4)], r1g.at[k, o - 1], ssem_1.at[1, k, o - 1], rsem_1.at[1, k, o - 1], at_y(o)
                )

    def second(k, n, buf, base, here, r1, s2, own, r2, got_1, got_2, at):
        for o in (1, 2, 3):
            got_1[k, o].wait_recv()
        for o in (2, 1, 3, 0):
            p = (here + o) % 4
            total = buf[k, base * 4 + p].astype(F32)
            for j in range(3):
                total = total + r1[k, j, p].astype(F32)
            if o:
                s2[k, p] = total.astype(BF16)
                got_2[k, o] = remote(s2.at[k, p], r2.at[k, o - 1], ssem_2.at[n, k, o - 1], rsem_2.at[n, k, o - 1], at(o))
            else:
                own[k] = total

    def second_p(k):
        second(k, 0, pbuf, x, y, r1p, s2p, ownp, r2p, got_1p, got_2p, at_y)

    def second_g(k):
        second(k, 1, gbuf, y, x, r1g, s2g, owng, r2g, got_1g, got_2g, at_x)

    got_h1, got_h2, got_q1, got_q2, got_d = {}, {}, {}, {}, {}
    hpos, qpos = x * 4 + y, y * 4 + x

    def activate(k):
        for o in (1, 2, 3):
            got_2p[k, o].wait_recv()
        p = ownp[k]
        for j in range(3):
            p = p + r2p[k, j].astype(F32)
        values, slopes = gelu_parts(p)
        hid[0, k, hpos] = values.astype(BF16)
        for o in (2, 1, 3):
            spot = hid.at[0, k, hpos]
            got_h1[k, o] = remote(spot, spot, ssem_h.at[0, k, o - 1], rsem_h.at[0, k, o - 1], at_y(o))
        for o in (1, 2, 3):
            got_2g[k, o].wait_recv()
        g = owng[k]
        for j in range(3):
            g = g + r2g[k, j].astype(F32)
        pre[0, k, qpos] = (g * slopes).astype(BF16)
        for o in (2, 1, 3):
            spot = pre.at[0, k, qpos]
            got_q1[k, o] = remote(spot, spot, ssem_q.at[0, k, o - 1], rsem_q.at[0, k, o - 1], at_x(o))

    def spread(k):
        for o in (1, 2, 3):
            got_h1[k, o].wait_recv()
        for o in (2, 1, 3):
            spot = hid.at[0, k, pl.ds(x * 4, 4)]
            got_h2[k, o] = remote(spot, spot, ssem_h.at[1, k, o - 1], rsem_h.at[1, k, o - 1], at_x(o))
        for o in (1, 2, 3):
            got_q1[k, o].wait_recv()
        for o in (2, 1, 3):
            spot = pre.at[0, k, pl.ds(y * 4, 4)]
            got_q2[k, o] = remote(spot, spot, ssem_q.at[1, k, o - 1], rsem_q.at[1, k, o - 1], at_y(o))

    def use_h(k):
        for o in (1, 2, 3):
            got_h2[k, o].wait_recv()
        got_d[0, k] = remote(hid.at[0, k], hid.at[1, k], ssem_d.at[0, k], rsem_d.at[0, k], partner)
        for n in range(3):

            def body(p, acc, n=n):
                xx, m = p // 2, p % 2
                fa = 16 * k + 8 * m + xx
                fb = fa + 4
                h = jnp.concatenate([hid[0, k, xx * 4 + 2 * m], hid[0, k, xx * 4 + 2 * m + 1]], axis=1)
                w = quad(block(dn, 2 * n, fa), block(dn, 2 * n + 1, fa), block(dn, 2 * n, fb), block(dn, 2 * n + 1, fb))
                return acc + dot(h, w)

            cols = slice(256 * n, 256 * n + 256)
            start = jnp.zeros((BLK, 256), F32) if k == 0 else acc_o[:, cols]
            acc_o[:, cols] = lax.fori_loop(0, 8, body, start)

    def use_q(k):
        for o in (1, 2, 3):
            got_q2[k, o].wait_recv()
        got_d[1, k] = remote(pre.at[0, k], pre.at[1, k], ssem_d.at[1, k], rsem_d.at[1, k], partner)
        for n in range(3):

            def body(p, acc, n=n):
                fa = 16 * k + 2 * p
                fb = fa + 1
                q = jnp.concatenate([pre[0, k, 2 * p], pre[0, k, 2 * p + 1]], axis=1)
                w = quad(block(up, 2 * n, fa), block(up, 2 * n, fb), block(up, 2 * n + 1, fa), block(up, 2 * n + 1, fb))
                return acc + dot_t(q, w)

            cols = slice(256 * n, 256 * n + 256)
            start = jnp.zeros((BLK, 256), F32) if k == 0 else acc_i[:, cols]
            acc_i[:, cols] = lax.fori_loop(0, 8, body, start)

    def scatter(n, acc, buf, recv):
        got = []
        buf[...] = acc[...].astype(BF16)
        for o in far_first:
            cc = (c + o) % NZ
            rows = pl.ds(pl.multiple_of(cc * ROWS, ROWS), ROWS)
            got.append(remote(buf.at[rows], recv.at[o - 1], ssem_z.at[n, o - 1], rsem_z.at[n, o - 1], at_z(o)))
        return got

    def gather_up(got, acc, recv, result):
        for copy in got:
            copy.wait_recv()
        total = acc[mine, :]
        for j in range(NZ - 1):
            total = total + recv[j].astype(F32)
        result[...] = total.astype(BF16)

    load_x.wait()
    for copy in got_x:
        copy.wait_recv()
    load_up.wait()
    make_p(0)
    load_g.wait()
    for copy in got_g:
        copy.wait_recv()
    load_dn.wait()
    make_g(0)
    got_d["x"] = remote(xs.at[0], xs.at[1], ssem_d.at[2, 0], rsem_d.at[2, 0], partner)
    got_d["g"] = remote(gs.at[0], gs.at[1], ssem_d.at[2, 1], rsem_d.at[2, 1], partner)
    make_p(1)
    second_p(0)
    make_g(1)
    second_g(0)
    make_p(2)
    second_p(1)
    activate(0)
    make_g(2)
    second_g(1)
    spread(0)
    second_p(2)
    activate(1)
    second_g(2)
    spread(1)
    use_h(0)
    use_q(0)
    activate(2)
    spread(2)
    use_h(1)
    use_q(1)
    got_d["x"].wait_recv()
    got_d["g"].wait_recv()
    for i in range(WB):
        cols = slice(BLK * i, BLK * i + BLK)
        for half in range(2):
            xt[i, :, BLK * half : BLK * half + BLK] = xs[half, :, cols].T
            gt[i, half] = gs[half, :, cols]
    use_h(2)
    got_o = scatter(0, acc_o, send_o, recv_o)
    use_q(2)
    got_i = scatter(1, acc_i, send_i, recv_i)

    alive = counts[0, 0]

    def grad_down(s, carry):
        slot = d * HALF + s
        number = slots[0, 0, slot]
        i, f = number // FB, number % FB
        k, yy, xx = f // 16, (f % 16) // 4, f % 4
        hpair = jnp.concatenate([hid[0, k, xx * 4 + yy], hid[1, k, xx * 4 + yy]], axis=0)
        gpair = jnp.concatenate([gt[i, 0], gt[i, 1]], axis=0)
        part = lax.dot_general(hpair, gpair, (((0,), (0,)), ((), ())), preferred_element_type=F32)
        live = jnp.where(slot < alive, 1.0, 0.0)
        gdn_v[s] = (part * live).astype(BF16)
        return carry

    def grad_up(s, carry):
        slot = d * HALF + s
        number = slots[0, 0, slot]
        i, f = number // FB, number % FB
        k, yy, xx = f // 16, (f % 16) // 4, f % 4
        qpair = jnp.concatenate([pre[0, k, yy * 4 + xx], pre[1, k, yy * 4 + xx]], axis=0)
        part = dot(xt[i], qpair)
        live = jnp.where(slot < alive, 1.0, 0.0)
        gup_v[s] = (part * live).astype(BF16)
        return carry

    stores = []

    def write(n, body, held, result):
        for part in range(3):
            lax.fori_loop(18 * part, 18 * part + 18, body, 0)
            span = pl.ds(18 * part, 18)
            copy = pltpu.make_async_copy(held.at[span], result.at[0, 0, span], osem.at[n, part])
            copy.start()
            stores.append(copy)

    for k in range(CHUNKS):
        got_d[0, k].wait_recv()
    write(0, grad_down, gdn_v, gdn_ref)
    gather_up(got_o, acc_o, recv_o, out_ref)
    for k in range(CHUNKS):
        got_d[1, k].wait_recv()
    write(1, grad_up, gup_v, gup_ref)
    gather_up(got_i, acc_i, recv_i, gin_ref)
    for copy in sends:
        copy.wait_send()
    for copy in stores:
        copy.wait()


def on_device(inputs, up_blocks, down_blocks, slots, counts, grad_out):
    places = jnp.arange(WB * FB, dtype=jnp.int32)
    order = jnp.arange(CAP, dtype=jnp.int32)
    held = (slots[0, 0][None, :] == places[:, None]) & (order < counts[0, 0])[None, :]
    inv = jnp.min(jnp.where(held, order[None, :], CAP), axis=1)
    smem = pl.BlockSpec(memory_space=pltpu.SMEM)
    vmem = pl.BlockSpec(memory_space=pltpu.VMEM)
    anym = pl.BlockSpec(memory_space=pl.ANY)
    dma = pltpu.SemaphoreType.DMA
    scratch = [
        pltpu.VMEM((CAP + 1, BLK, BLK), BF16),
        pltpu.VMEM((CAP + 1, BLK, BLK), BF16),
        pltpu.VMEM((2, BLK, WB * BLK), BF16),
        pltpu.VMEM((2, BLK, WB * BLK), BF16),
        pltpu.VMEM((WB, BLK, 2 * BLK), BF16),
        pltpu.VMEM((WB, 2, BLK, BLK), BF16),
        pltpu.VMEM((CHUNKS, 16, BLK, BLK), BF16),
        pltpu.VMEM((CHUNKS, 16, BLK, BLK), BF16),
        pltpu.VMEM((CHUNKS, 3, 4, BLK, BLK), BF16),
        pltpu.VMEM((CHUNKS, 3, 4, BLK, BLK), BF16),
        pltpu.VMEM((CHUNKS, 4, BLK, BLK), BF16),
        pltpu.VMEM((CHUNKS, 4, BLK, BLK), BF16),
        pltpu.VMEM((CHUNKS, BLK, BLK), F32),
        pltpu.VMEM((CHUNKS, BLK, BLK), F32),
        pltpu.VMEM((CHUNKS, 3, BLK, BLK), BF16),
        pltpu.VMEM((CHUNKS, 3, BLK, BLK), BF16),
        pltpu.VMEM((2, CHUNKS, 16, BLK, BLK), BF16),
        pltpu.VMEM((2, CHUNKS, 16, BLK, BLK), BF16),
        pltpu.VMEM((BLK, WB * BLK), F32),
        pltpu.VMEM((BLK, WB * BLK), F32),
        pltpu.VMEM((BLK, WB * BLK), BF16),
        pltpu.VMEM((BLK, WB * BLK), BF16),
        pltpu.VMEM((NZ - 1, ROWS, WB * BLK), BF16),
        pltpu.VMEM((NZ - 1, ROWS, WB * BLK), BF16),
        pltpu.VMEM((HALF, BLK, BLK), BF16),
        pltpu.VMEM((HALF, BLK, BLK), BF16),
        dma((2,)),
        dma((2,)),
        dma((2, NZ - 1)),
        dma((2, NZ - 1)),
        dma((2, CHUNKS, 3)),
        dma((2, CHUNKS, 3)),
        dma((2, CHUNKS, 3)),
        dma((2, CHUNKS, 3)),
        dma((2, CHUNKS, 3)),
        dma((2, CHUNKS, 3)),
        dma((2, CHUNKS, 3)),
        dma((2, CHUNKS, 3)),
        dma((3, CHUNKS)),
        dma((3, CHUNKS)),
        dma((2, NZ - 1)),
        dma((2, NZ - 1)),
        dma((2, 3)),
    ]
    return pl.pallas_call(
        kernel,
        out_shape=(
            jax.ShapeDtypeStruct((ROWS, WB * BLK), BF16),
            jax.ShapeDtypeStruct((ROWS, WB * BLK), BF16),
            jax.ShapeDtypeStruct((1, 1, HALF, BLK, BLK), BF16),
            jax.ShapeDtypeStruct((1, 1, HALF, BLK, BLK), BF16),
        ),
        in_specs=[smem, smem, smem, anym, anym, anym, anym],
        out_specs=(vmem, vmem, anym, anym),
        scratch_shapes=scratch,
        compiler_params=pltpu.CompilerParams(
            collective_id=0, has_side_effects=True, vmem_limit_bytes=52 * 1024 * 1024
        ),
    )(inv, slots, counts, inputs, grad_out, up_blocks, down_blocks)


def solution(mesh):
    return jax.shard_map(
        on_device,
        mesh=mesh,
        in_specs=(
            P(("depth", "col"), "row"),
            P("row", "col", None, None, None),
            P("row", "col", None, None, None),
            P("row", "col", None),
            P("row", "col"),
            P(("depth", "col"), "row"),
        ),
        out_specs=(
            P(("depth", "col"), "row"),
            P(("depth", "col"), "row"),
            P("row", "col", "depth", None, None),
            P("row", "col", "depth", None, None),
        ),
        check_vma=False,
    )
```

time: 519 us -> 116 us (0.22)
  waiting for transfers between devices: 312 us -> 0 us
  Pallas kernels: 0 us -> 107 us
  local copies, waits for them, and re-layouts: 77.2 us -> 6.66 us
  matrix products: 68.9 us -> 0 us
  blocking collectives: 41.7 us -> 0 us
  between operations: 15.6 us -> 1.31 us
    unnamed x10 -> x0, waiting for transfers between devices: 173 us -> none
    pallas_call x0 -> x1, Pallas kernels: none -> 107 us  [on_device(): pl.pallas_call(kernel, out_shape=(jax.ShapeDtypeStruct((ROWS, WB * BLK),...]
    all_gather x2 -> x0, waiting for transfers between devices: 96.1 us -> none  [the longest x1 48.9 us: on_device(): hidden = lax.all_gather(hidden_share, 'row', axis=0, tiled=True)]
    dot_general x10 -> x0, matrix products: 68.9 us -> none  [the longest x4 22.9 us: spread_blocks(): jnp.einsum('tsb,sf->tfb', products, placing, precision=lax.Precision.HIGH...]
    reduce_scatter x2 -> x0, waiting for transfers between devices: 43.2 us -> none  [the longest x1 22.1 us: on_device(): lax.psum_scatter(part_up.astype(jnp.bfloat16), 'depth', scatter_dimension...]
    all_gather x2 -> x0, blocking collectives: 41.7 us -> none  [the longest x1 23.4 us: on_device(): lax.all_gather(grad_out, 'col', axis=0, tiled=True)]
    transpose x6 -> x0, local copies, waits for them, and re-layouts: 36.4 us -> none  [the longest x1 8.13 us: on_device(): jnp.einsum('tsb,sba->tsa', chosen, weight_two, preferred_element_type=jnp...]
    gather x4 -> x0, local copies, waits for them, and re-layouts: 11.2 us -> none  [pick_blocks(): return rows_in.reshape(height, -1, block_size)[:, block_ids, :]]
  transfers between devices with their start and end apart: 7 -> 0, of which waited for: 6 -> 0; matrix products, arithmetic and copies ran while one was open for 8% -> 0% of each run, Pallas kernels for 0% -> 0%
where the time goes in v1:
time: 116 us
  Pallas kernels  107 us (92%)
  local copies, waits for them, and re-layouts  6.66 us (6%)
  between operations  1.31 us (1%)
    pallas_call x1, Pallas kernels, on_device(): pl.pallas_call(kernel, out_shape=(jax.ShapeDtypeStruct((ROWS, WB * BLK),...  107 us
    unnamed x12, local copies, waits for them, and re-layouts  6.66 us

profile of v1, /device:TPU:1, one launch (start us, length us, event | category | flops | bytes accessed | tf_op | source)
XLA Modules:
  0.0 116.2 jit_solution(572655905893054300)
XLA Ops:
  1.3 0.8 select_reduce_fusion.inv
  2.1 0.0 copy-start
  2.1 0.7 copy-done
  2.8 0.0 copy-start.1
  2.8 0.7 copy-done.1
  3.6 0.0 copy-start.2
  3.6 0.7 copy-done.2
  4.2 107.4 %shard_map.93 = (bf16[16,768]{1,0:T(8,128)(2,1)S(1)}, bf16[16,768]{1,0:T(8,128)(2,1)S(1)}, bf16[1,1,54,128,128]{4,3,2,1,0:T(8,128)(2,1)S(1)}, bf16[1,1,54,128,128]{4,3,2,1,0:T(8,128)(2,1)}) custom-call(s32[288]{0:T(512)S(1)} %select_reduce_fusion.inv, s32[1,1,108]{2,1,0:T(1,128)S(1)} %copy-done.2, s32[1,1]{1,0:T(1,128)} %copy.14.counts, ...), custom_call_target="tpu_custom_call" | custom-call | tf_op jit(solution)/shard_map/pallas_call | solution.py:410
  111.6 0.6 copy.15
  112.3 0.6 copy.16
  112.9 0.0 copy-start.3
  112.9 1.2 %copy.17 = bf16[1,1,54,128,128]{4,3,2,1,0:T(8,128)(2,1)} copy(bf16[1,1,54,128,128]{4,3,2,1,0:T(8,128)(2,1)S(1)} %get-tuple-element.10) | data formatting | bytes 3538944
  114.1 0.9 copy-done.3
  115.0 1.2 %copy.18 = bf16[1,1,54,128,128]{4,3,2,1,0:T(8,128)(2,1)} copy(bf16[1,1,54,128,128]{4,3,2,1,0:T(8,128)(2,1)S(1)} %copy-done.3) | data formatting | bytes 3538944
  (1 shorter events, 0.0 us)
Async XLA Ops:
  2.1 0.7 copy-start
  2.8 0.7 copy-start.1
  3.6 0.7 copy-start.2
  112.9 2.1 %copy-start.3 = (bf16[1,1,54,128,128]{4,3,2,1,0:T(8,128)(2,1)S(1)}, bf16[1,1,54,128,128]{4,3,2,1,0:T(8,128)(2,1)}, u32[]{:S(2)}) copy-start(bf16[1,1,54,128,128]{4,3,2,1,0:T(8,128)(2,1)} %get-tuple-element.11) | copy-start | bytes 5308420

commit v2 on v1

--- a/solution.py
+++ b/solution.py
@@ -42,12 +42,12 @@
 
 
 def kernel(
-    inv, slots, counts, x_in, g_in, up_in, dn_in,
+    inv_in, slots_in, counts_in, x_in, g_in, up_in, dn_in,
     out_ref, gin_ref, gup_ref, gdn_ref,
-    up, dn, xs, gs, xt, gt, pbuf, gbuf, r1p, r1g, s2p, s2g, ownp, owng, r2p, r2g,
-    hid, pre, acc_o, acc_i, send_o, send_i, recv_o, recv_i, gup_v, gdn_v,
+    inv, slots, counts, up, dn, xs, gs, xt, gt, pbuf, gbuf, r1p, r1g, s2p, s2g, ownp, owng, r2p, r2g,
+    hid, pre, acc_o, acc_i, send_o, send_i, recv_o, recv_i,
     wsem, lsem, ssem_a, rsem_a, ssem_1, rsem_1, ssem_2, rsem_2, ssem_h, rsem_h, ssem_q, rsem_q,
-    ssem_d, rsem_d, ssem_z, rsem_z, osem,
+    ssem_d, rsem_d, ssem_z, rsem_z, tsem,
 ):
     d, r, c = lax.axis_index("depth"), lax.axis_index("row"), lax.axis_index("col")
     y, x = r // NX, r % NX
@@ -77,6 +77,12 @@
     mine = pl.ds(pl.multiple_of(c * ROWS, ROWS), ROWS)
     load_x = pltpu.make_async_copy(x_in, xs.at[0, mine], lsem.at[0])
     load_g = pltpu.make_async_copy(g_in, gs.at[0, mine], lsem.at[1])
+    tables = [
+        pltpu.make_async_copy(source, held, tsem.at[n])
+        for n, (source, held) in enumerate(((inv_in, inv), (slots_in, slots), (counts_in, counts)))
+    ]
+    for copy in tables:
+        copy.start()
     load_x.start()
     load_g.start()
     load_up.start()
@@ -122,14 +128,11 @@
         for o in (2, 1, 3, 0):
             xx = (x + o) % NX
 
-            def body(m, carry, xx=xx):
+            for m in range(2):
                 fa = 16 * k + 8 * m + xx
                 acc = pair_p(fa, fa + NX).astype(BF16)
                 pbuf[k, xx * 4 + 2 * m] = acc[:, :BLK]
                 pbuf[k, xx * 4 + 2 * m + 1] = acc[:, BLK:]
-                return carry
-
-            lax.fori_loop(0, 2, body, 0)
             if o:
                 got_1p[k, o] = remote(
                     pbuf.at[k, pl.ds(xx * 4, 4)], r1p.at[k, o - 1], ssem_1.at[0, k, o - 1], rsem_1.at[0, k, o - 1], at_x(o)
@@ -139,14 +142,11 @@
         for o in (2, 1, 3, 0):
             yy = (y + o) % NY
 
-            def body(m, carry, yy=yy):
+            for m in range(2):
                 fa = 16 * k + 4 * yy + 2 * m
                 acc = pair_g(fa, fa + 1).astype(BF16)
                 gbuf[k, yy * 4 + 2 * m] = acc[:, :BLK]
                 gbuf[k, yy * 4 + 2 * m + 1] = acc[:, BLK:]
-                return carry
-
-            lax.fori_loop(0, 2, body, 0)
             if o:
                 got_1g[k, o] = remote(
                     gbuf.at[k, pl.ds(yy * 4, 4)], r1g.at[k, o - 1], ssem_1.at[1, k, o - 1], rsem_1.at[1, k, o - 1], at_y(o)
@@ -212,36 +212,33 @@
         for o in (1, 2, 3):
             got_h2[k, o].wait_recv()
         got_d[0, k] = remote(hid.at[0, k], hid.at[1, k], ssem_d.at[0, k], rsem_d.at[0, k], partner)
+        places = [(xx, yy) for xx in range(NX) for yy in range(NY)]
+        h = jnp.concatenate([hid[0, k, xx * 4 + yy] for xx, yy in places], axis=1)
         for n in range(3):
-
-            def body(p, acc, n=n):
-                xx, m = p // 2, p % 2
-                fa = 16 * k + 8 * m + xx
-                fb = fa + 4
-                h = jnp.concatenate([hid[0, k, xx * 4 + 2 * m], hid[0, k, xx * 4 + 2 * m + 1]], axis=1)
-                w = quad(block(dn, 2 * n, fa), block(dn, 2 * n + 1, fa), block(dn, 2 * n, fb), block(dn, 2 * n + 1, fb))
-                return acc + dot(h, w)
-
             cols = slice(256 * n, 256 * n + 256)
-            start = jnp.zeros((BLK, 256), F32) if k == 0 else acc_o[:, cols]
-            acc_o[:, cols] = lax.fori_loop(0, 8, body, start)
+            w = jnp.concatenate(
+                [
+                    jnp.concatenate([block(dn, 2 * n + u, 16 * k + 4 * yy + xx) for u in range(2)], axis=1)
+                    for xx, yy in places
+                ],
+                axis=0,
+            )
+            part = dot(h, w)
+            acc_o[:, cols] = part if k == 0 else acc_o[:, cols] + part
 
     def use_q(k):
         for o in (1, 2, 3):
             got_q2[k, o].wait_recv()
         got_d[1, k] = remote(pre.at[0, k], pre.at[1, k], ssem_d.at[1, k], rsem_d.at[1, k], partner)
+        q = jnp.concatenate([pre[0, k, p] for p in range(16)], axis=1)
         for n in range(3):
-
-            def body(p, acc, n=n):
-                fa = 16 * k + 2 * p
-                fb = fa + 1
-                q = jnp.concatenate([pre[0, k, 2 * p], pre[0, k, 2 * p + 1]], axis=1)
-                w = quad(block(up, 2 * n, fa), block(up, 2 * n, fb), block(up, 2 * n + 1, fa), block(up, 2 * n + 1, fb))
-                return acc + dot_t(q, w)
-
             cols = slice(256 * n, 256 * n + 256)
-            start = jnp.zeros((BLK, 256), F32) if k == 0 else acc_i[:, cols]
-            acc_i[:, cols] = lax.fori_loop(0, 8, body, start)
+            w = jnp.concatenate(
+                [jnp.concatenate([block(up, 2 * n + u, 16 * k + p) for p in range(16)], axis=1) for u in range(2)],
+                axis=0,
+            )
+            part = dot_t(q, w)
+            acc_i[:, cols] = part if k == 0 else acc_i[:, cols] + part
 
     def scatter(n, acc, buf, recv):
         got = []
@@ -264,34 +261,29 @@
     for copy in got_x:
         copy.wait_recv()
     load_up.wait()
-    make_p(0)
+    for copy in tables:
+        copy.wait()
+    for k in range(CHUNKS):
+        make_p(k)
     load_g.wait()
     for copy in got_g:
         copy.wait_recv()
     load_dn.wait()
-    make_g(0)
+    for k in range(CHUNKS):
+        make_g(k)
     got_d["x"] = remote(xs.at[0], xs.at[1], ssem_d.at[2, 0], rsem_d.at[2, 0], partner)
     got_d["g"] = remote(gs.at[0], gs.at[1], ssem_d.at[2, 1], rsem_d.at[2, 1], partner)
-    make_p(1)
     second_p(0)
-    make_g(1)
     second_g(0)
-    make_p(2)
     second_p(1)
+    second_g(1)
     activate(0)
-    make_g(2)
-    second_g(1)
+    second_p(2)
+    second_g(2)
+    activate(1)
     spread(0)
-    second_p(2)
-    activate(1)
-    second_g(2)
+    activate(2)
     spread(1)
-    use_h(0)
-    use_q(0)
-    activate(2)
-    spread(2)
-    use_h(1)
-    use_q(1)
     got_d["x"].wait_recv()
     got_d["g"].wait_recv()
     for i in range(WB):
@@ -299,6 +291,11 @@
         for half in range(2):
             xt[i, :, BLK * half : BLK * half + BLK] = xs[half, :, cols].T
             gt[i, half] = gs[half, :, cols]
+    spread(2)
+    use_h(0)
+    use_q(0)
+    use_h(1)
+    use_q(1)
     use_h(2)
     got_o = scatter(0, acc_o, send_o, recv_o)
     use_q(2)
@@ -315,7 +312,7 @@
         gpair = jnp.concatenate([gt[i, 0], gt[i, 1]], axis=0)
         part = lax.dot_general(hpair, gpair, (((0,), (0,)), ((), ())), preferred_element_type=F32)
         live = jnp.where(slot < alive, 1.0, 0.0)
-        gdn_v[s] = (part * live).astype(BF16)
+        gdn_ref[0, 0, s] = (part * live).astype(BF16)
         return carry
 
     def grad_up(s, carry):
@@ -326,30 +323,28 @@
         qpair = jnp.concatenate([pre[0, k, yy * 4 + xx], pre[1, k, yy * 4 + xx]], axis=0)
         part = dot(xt[i], qpair)
         live = jnp.where(slot < alive, 1.0, 0.0)
-        gup_v[s] = (part * live).astype(BF16)
+        gup_ref[0, 0, s] = (part * live).astype(BF16)
         return carry
-
-    stores = []
-
-    def write(n, body, held, result):
-        for part in range(3):
-            lax.fori_loop(18 * part, 18 * part + 18, body, 0)
-            span = pl.ds(18 * part, 18)
-            copy = pltpu.make_async_copy(held.at[span], result.at[0, 0, span], osem.at[n, part])
-            copy.start()
-            stores.append(copy)
 
     for k in range(CHUNKS):
         got_d[0, k].wait_recv()
-    write(0, grad_down, gdn_v, gdn_ref)
+    for part in range(3):
+        lax.fori_loop(18 * part, 18 * part + 18, grad_down, 0, unroll=18)
     gather_up(got_o, acc_o, recv_o, out_ref)
     for k in range(CHUNKS):
         got_d[1, k].wait_recv()
-    write(1, grad_up, gup_v, gup_ref)
+    for part in range(3):
+        lax.fori_loop(18 * part, 18 * part + 18, grad_up, 0, unroll=18)
     gather_up(got_i, acc_i, recv_i, gin_ref)
     for copy in sends:
         copy.wait_send()
-    for copy in stores:
+
+
+def write_out(*refs):
+    copies = [pltpu.make_async_copy(refs[n], refs[n + 4], refs[8].at[n]) for n in range(4)]
+    for copy in copies:
+        copy.start()
+    for copy in copies:
         copy.wait()
 
 
@@ -358,11 +353,13 @@
     order = jnp.arange(CAP, dtype=jnp.int32)
     held = (slots[0, 0][None, :] == places[:, None]) & (order < counts[0, 0])[None, :]
     inv = jnp.min(jnp.where(held, order[None, :], CAP), axis=1)
-    smem = pl.BlockSpec(memory_space=pltpu.SMEM)
     vmem = pl.BlockSpec(memory_space=pltpu.VMEM)
-    anym = pl.BlockSpec(memory_space=pl.ANY)
+    hbm = pl.BlockSpec(memory_space=pltpu.HBM)
     dma = pltpu.SemaphoreType.DMA
     scratch = [
+        pltpu.SMEM((WB * FB,), jnp.int32),
+        pltpu.SMEM((1, 1, CAP), jnp.int32),
+        pltpu.SMEM((1, 1), jnp.int32),
         pltpu.VMEM((CAP + 1, BLK, BLK), BF16),
         pltpu.VMEM((CAP + 1, BLK, BLK), BF16),
         pltpu.VMEM((2, BLK, WB * BLK), BF16),
@@ -387,8 +384,6 @@
         pltpu.VMEM((BLK, WB * BLK), BF16),
         pltpu.VMEM((NZ - 1, ROWS, WB * BLK), BF16),
         pltpu.VMEM((NZ - 1, ROWS, WB * BLK), BF16),
-        pltpu.VMEM((HALF, BLK, BLK), BF16),
-        pltpu.VMEM((HALF, BLK, BLK), BF16),
         dma((2,)),
         dma((2,)),
         dma((2, NZ - 1)),
@@ -405,23 +400,27 @@
         dma((3, CHUNKS)),
         dma((2, NZ - 1)),
         dma((2, NZ - 1)),
-        dma((2, 3)),
+        dma((3,)),
     ]
-    return pl.pallas_call(
+    shapes = (
+        jax.ShapeDtypeStruct((ROWS, WB * BLK), BF16),
+        jax.ShapeDtypeStruct((ROWS, WB * BLK), BF16),
+        jax.ShapeDtypeStruct((1, 1, HALF, BLK, BLK), BF16),
+        jax.ShapeDtypeStruct((1, 1, HALF, BLK, BLK), BF16),
+    )
+    results = pl.pallas_call(
         kernel,
-        out_shape=(
-            jax.ShapeDtypeStruct((ROWS, WB * BLK), BF16),
-            jax.ShapeDtypeStruct((ROWS, WB * BLK), BF16),
-            jax.ShapeDtypeStruct((1, 1, HALF, BLK, BLK), BF16),
-            jax.ShapeDtypeStruct((1, 1, HALF, BLK, BLK), BF16),
-        ),
-        in_specs=[smem, smem, smem, anym, anym, anym, anym],
-        out_specs=(vmem, vmem, anym, anym),
+        out_shape=shapes,
+        in_specs=[hbm] * 7,
+        out_specs=(vmem,) * 4,
         scratch_shapes=scratch,
         compiler_params=pltpu.CompilerParams(
-            collective_id=0, has_side_effects=True, vmem_limit_bytes=52 * 1024 * 1024
+            collective_id=0, has_side_effects=True, vmem_limit_bytes=48 * 1024 * 1024
         ),
     )(inv, slots, counts, inputs, grad_out, up_blocks, down_blocks)
+    return pl.pallas_call(
+        write_out, out_shape=shapes, in_specs=[vmem] * 4, out_specs=(hbm,) * 4, scratch_shapes=[dma((4,))]
+    )(*results)
 
 
 def solution(mesh):

time: 116 us -> 90 us (0.78)
  Pallas kernels: 107 us -> 81.9 us
    pallas_call x1 -> x2, Pallas kernels: 107 us -> 81.9 us  [the longest x1 78 us: on_device(): pl.pallas_call(kernel, out_shape=shapes, in_specs=[hbm] * 7, out_specs=(v...]
    unnamed x12 -> x14, local copies, waits for them, and re-layouts: 6.66 us -> 5.76 us
where the time goes in v2:
time: 90 us; the launch traced here: 89.7 us
  Pallas kernels  81.9 us (91%)
  local copies, waits for them, and re-layouts  5.76 us (6%)
  between operations  1.32 us (1%)
    pallas_call x1, Pallas kernels, on_device(): pl.pallas_call(kernel, out_shape=shapes, in_specs=[hbm] * 7, out_specs=(v...  78 us
    unnamed x14, local copies, waits for them, and re-layouts  5.76 us
    pallas_call x1, Pallas kernels, on_device(): pl.pallas_call(write_out, out_shape=shapes, in_specs=[vmem] * 4, out_spec...  3.88 us

profile of v2, /device:TPU:1, one launch (start us, length us, event | category | flops | bytes accessed | tf_op | source)
XLA Modules:
  0.0 89.7 jit_solution(7119486036266372860)
XLA Ops:
  1.3 0.8 select_reduce_fusion.inv_in
  2.1 0.0 copy-start.4
  2.1 0.7 copy-done.4
  2.8 0.0 copy-start.5
  2.8 0.7 copy-done.5
  3.6 0.0 copy-start.6
  3.6 0.7 copy-done.6
  4.2 78.0 %shard_map.93 = (bf16[16,768]{1,0:T(8,128)(2,1)S(1)}, bf16[16,768]{1,0:T(8,128)(2,1)S(1)}, bf16[1,1,54,128,128]{4,3,2,1,0:T(8,128)(2,1)S(1)}, bf16[1,1,54,128,128]{4,3,2,1,0:T(8,128)(2,1)S(1)}) custom-call(s32[288]{0:T(512)S(1)} %select_reduce_fusion.inv_in, s32[1,1,108]{2,1,0:T(1,128)S(1)} %copy-done.6, s32[1,1]{1,0:T(1,128)} %copy.10.counts_in, ...), custom_call_target="tpu_custom_call" | custom-call | tf_op jit(solution)/shard_map/pallas_call | solution.py:411
  82.2 0.0 copy-start
  82.2 1.2 %copy-done = bf16[1,1,54,128,128]{4,3,2,1,0:T(8,128)(2,1)} copy-done((bf16[1,1,54,128,128]{4,3,2,1,0:T(8,128)(2,1)}, bf16[1,1,54,128,128]{4,3,2,1,0:T(8,128)(2,1)S(1)}, u32[]{:S(2)}) %copy-start) | copy-done | bytes 1769496
  83.5 0.0 copy-start.1
  83.5 1.2 %copy-done.1 = bf16[1,1,54,128,128]{4,3,2,1,0:T(8,128)(2,1)} copy-done((bf16[1,1,54,128,128]{4,3,2,1,0:T(8,128)(2,1)}, bf16[1,1,54,128,128]{4,3,2,1,0:T(8,128)(2,1)S(1)}, u32[]{:S(2)}) %copy-start.1) | copy-done | bytes 1769496
  84.7 0.0 copy-start.2
  84.7 0.6 copy-done.2
  85.3 0.0 copy-start.3
  85.3 0.6 copy-done.3
  85.9 3.9 %shard_map.94 = (bf16[16,768]{1,0:T(8,128)(2,1)}, bf16[16,768]{1,0:T(8,128)(2,1)}, bf16[1,1,54,128,128]{4,3,2,1,0:T(8,128)(2,1)}, bf16[1,1,54,128,128]{4,3,2,1,0:T(8,128)(2,1)}) custom-call(bf16[16,768]{1,0:T(8,128)(2,1)} %copy-done.2, bf16[16,768]{1,0:T(8,128)(2,1)} %copy-done.3, bf16[1,1,54,128,128]{4,3,2,1,0:T(8,128)(2,1)} %copy-done, ...), custom_call_target="tpu_custom_call" | custom-call | tf_op jit(solution)/shard_map/pallas_call | solution.py:421
  (1 shorter events, 0.0 us)
Async XLA Ops:
  2.1 0.7 copy-start.4
  2.8 0.7 copy-start.5
  3.6 0.7 copy-start.6
  82.2 1.2 %copy-start = (bf16[1,1,54,128,128]{4,3,2,1,0:T(8,128)(2,1)}, bf16[1,1,54,128,128]{4,3,2,1,0:T(8,128)(2,1)S(1)}, u32[]{:S(2)}) copy-start(bf16[1,1,54,128,128]{4,3,2,1,0:T(8,128)(2,1)S(1)} %get-tuple-element.10.refs_2_) | copy-start | bytes 5308420
  83.5 1.2 %copy-start.1 = (bf16[1,1,54,128,128]{4,3,2,1,0:T(8,128)(2,1)}, bf16[1,1,54,128,128]{4,3,2,1,0:T(8,128)(2,1)S(1)}, u32[]{:S(2)}) copy-start(bf16[1,1,54,128,128]{4,3,2,1,0:T(8,128)(2,1)S(1)} %get-tuple-element.11.refs_3_) | copy-start | bytes 5308420
  84.7 0.6 copy-start.2
  85.3 0.6 copy-start.3

commit v3 on v2

v3 whole, which is shorter than its diff:
```python
import jax
import jax.numpy as jnp
from jax import lax
from jax.experimental import pallas as pl
from jax.experimental.pallas import tpu as pltpu
from jax.sharding import PartitionSpec as P

MESH = pl.DeviceIdType.MESH
F32, BF16 = jnp.float32, jnp.bfloat16
BLK, CAP, HALF = 128, 108, 54
WB, FB = 6, 48
NX, NY, NZ = 4, 4, 8
CHUNKS = 3
ROWS = 16
ORDER = (
    "w00m00m01m02w10m10m11f00f01m12f02f10f11s00s01s02f12x00x10s10",
    "s11a00a01s12a02t00a10d00d01a11a12d02d10r00r01d11d12r02r10u00",
    "r11u01r12u02z00u10u11u12z10g00c00g10c10",
)
ORDER = [part[i : i + 3] for part in ORDER for i in range(0, len(part), 3)]

root_coeff = 0.7978845608
cube_coeff = 0.044715


def gelu_parts(preact):
    cubed = preact * preact * preact
    tangent = jnp.tanh(root_coeff * (preact + cube_coeff * cubed))
    values = 0.5 * preact * (1.0 + tangent)
    slopes = 0.5 * (1.0 + tangent) + 0.5 * preact * (1.0 - tangent * tangent) * root_coeff * (
        1.0 + 3.0 * cube_coeff * preact * preact
    )
    return (values, slopes)


def dot(a, b):
    return lax.dot_general(a, b, (((1,), (0,)), ((), ())), preferred_element_type=F32)


def dot_t(a, b):
    return lax.dot_general(a, b, (((1,), (1,)), ((), ())), preferred_element_type=F32)


def quad(a, b, c, d):
    return jnp.concatenate(
        [jnp.concatenate([a, b], axis=1), jnp.concatenate([c, d], axis=1)], axis=0
    )


def kernel(
    inv_in, slots_in, counts_in, x_in, g_in, up_in, dn_in,
    out_ref, gin_ref, gup_ref, gdn_ref,
    inv, slots, counts, up, dn, xs, gs, xt, gt, farp, farg, nearp, nearg, keptp, keptg, thrup, thrug, joinp, joing, r1p, r1g, s2p, s2g, ownp, owng, slopes, r2p, r2g,
    hid, pre, acc_o, acc_i, send_o, send_i, recv_o, recv_i,
    wsem, lsem, ssem_a, rsem_a, ssem_1, rsem_1, ssem_2, rsem_2, ssem_h, rsem_h, ssem_q, rsem_q, ssem_h4, rsem_h4, ssem_q4, rsem_q4,
    ssem_d, rsem_d, ssem_z, rsem_z, tsem,
):
    d, r, c = lax.axis_index("depth"), lax.axis_index("row"), lax.axis_index("col")
    y, x = r // NX, r % NX
    sends = []

    def at_x(o):
        return (d, y * NX + (x + o) % NX, c)

    def at_y(o):
        return (d, ((y + o) % NY) * NX + x, c)

    def at_z(o):
        return (d, r, (c + o) % NZ)

    partner = (1 - d, r, c)

    def remote(src, dst, ssem, rsem, device):
        copy = pltpu.make_async_remote_copy(
            src_ref=src, dst_ref=dst, send_sem=ssem, recv_sem=rsem, device_id=device, device_id_type=MESH
        )
        copy.start()
        sends.append(copy)
        return copy

    load_up = pltpu.make_async_copy(up_in.at[0, 0], up.at[pl.ds(0, CAP)], wsem.at[0])
    load_dn = pltpu.make_async_copy(dn_in.at[0, 0], dn.at[pl.ds(0, CAP)], wsem.at[1])
    mine = pl.ds(pl.multiple_of(c * ROWS, ROWS), ROWS)
    load_x = pltpu.make_async_copy(x_in, xs.at[0, mine], lsem.at[0])
    load_g = pltpu.make_async_copy(g_in, gs.at[0, mine], lsem.at[1])
    tables = [
        pltpu.make_async_copy(source, held, tsem.at[n])
        for n, (source, held) in enumerate(((inv_in, inv), (slots_in, slots), (counts_in, counts)))
    ]
    for copy in tables:
        copy.start()
    load_x.start()
    load_g.start()
    load_up.start()
    load_dn.start()
    up[CAP] = jnp.zeros((BLK, BLK), BF16)
    dn[CAP] = jnp.zeros((BLK, BLK), BF16)

    barrier = pltpu.get_barrier_semaphore()
    peers = [at_x(o) for o in (1, 2, 3)] + [at_y(o) for o in (1, 2, 3)]
    peers += [at_z(o) for o in range(1, NZ)] + [partner]
    for peer in peers:
        pl.semaphore_signal(barrier, inc=1, device_id=peer, device_id_type=MESH)
    pl.semaphore_wait(barrier, len(peers))

    got_x, got_g = [], []
    for n, (load, held, got) in enumerate(((load_x, xs, got_x), (load_g, gs, got_g))):
        load.wait()
        spot = held.at[0, mine]
        for o in (4, 3, 5, 2, 6, 1, 7):
            got.append(remote(spot, spot, ssem_a.at[n, o], rsem_a.at[n, o], at_z(o)))

    def block(weights, i, f):
        return weights[inv[i * FB + f]]

    def pair_p(fa, fb):
        acc = None
        for kk in range(3):
            w = quad(block(up, 2 * kk, fa), block(up, 2 * kk, fb), block(up, 2 * kk + 1, fa), block(up, 2 * kk + 1, fb))
            term = dot(xs[0, :, 256 * kk : 256 * kk + 256], w)
            acc = term if acc is None else acc + term
        return acc

    def pair_g(fa, fb):
        acc = None
        for kk in range(3):
            w = quad(block(dn, 2 * kk, fa), block(dn, 2 * kk + 1, fa), block(dn, 2 * kk, fb), block(dn, 2 * kk + 1, fb))
            term = dot_t(gs[0, :, 256 * kk : 256 * kk + 256], w)
            acc = term if acc is None else acc + term
        return acc

    far, near_out, kept, through, joined = (farp, farg), (nearp, nearg), (keptp, keptg), (thrup, thrug), (joinp, joing)
    first_in, second_out, own, second_in = (r1p, r1g), (s2p, s2g), (ownp, owng), (r2p, r2g)
    gathered, gsem, gsem4 = (hid, pre), ((ssem_h, rsem_h), (ssem_q, rsem_q)), ((ssem_h4, rsem_h4), (ssem_q4, rsem_q4))
    got_1, got_2, got_3, got_4, got_d = {}, {}, {}, {}, {}

    def x_first(n, k):
        return (n + k) % 2 == 0

    def axes(n, k):
        return (x, at_x, y, at_y) if x_first(n, k) else (y, at_y, x, at_x)

    def hidden_block(n, k, a, b):
        return 16 * k + (4 * b + a if x_first(n, k) else 4 * a + b)

    def send_1(n, k, i, src, dst, at):
        got_1[n, k, i] = remote(src, dst, ssem_1.at[n, k, i], rsem_1.at[n, k, i], at(3 if i % 2 else 1))

    def make(n, k):
        here, at, _, _ = axes(n, k)

        def product(o, m):
            a = (here + o) % 4
            return (pair_p, pair_g)[n](hidden_block(n, k, a, 2 * m), hidden_block(n, k, a, 2 * m + 1))

        def keep(ref, where, value):
            ref[where] = value[:, :BLK].astype(ref.dtype)
            ref[(*where[:-1], where[-1] + 1)] = value[:, BLK:].astype(ref.dtype)

        for m in range(2):
            keep(far[n], (k, 2 * m), product(2, m))
            send_1(n, k, m, far[n].at[k, pl.ds(2 * m, 2)], through[n].at[k, m], at)
        for way, o in ((0, 1), (1, 3)):
            keep(near_out[n], (k, way, 0), product(o, 1 - way))
            send_1(n, k, 2 + way, near_out[n].at[k, way, pl.ds(0, 2)], first_in[n].at[k, 1 + way, pl.ds(2 - 2 * way, 2)], at)
        for way, o in ((0, 1), (1, 3)):
            keep(kept[n], (k, 4 + 2 * way), product(o, way))
        for m in range(2):
            keep(kept[n], (k, 2 * m), product(0, m))

    def forward(n, k):
        _, at, _, _ = axes(n, k)
        for way in range(2):
            got_1[n, k, way].wait_recv()
            for i in range(2):
                total = kept[n][k, 4 + 2 * way + i] + through[n][k, way, i].astype(F32)
                joined[n][k, way, i] = total.astype(BF16)
            send_1(n, k, 4 + way, joined[n].at[k, way], first_in[n].at[k, 1 + way, pl.ds(2 * way, 2)], at)

    def second(n, k):
        _, _, here, at = axes(n, k)
        for i in range(2, 6):
            got_1[n, k, i].wait_recv()
        for o in (2, 1, 3, 0):
            b = (here + o) % 4
            total = kept[n][k, b]
            for i in range(1, 3):
                total = total + first_in[n][k, i, b].astype(F32)
            if o:
                second_out[n][k, b] = total.astype(BF16)
                got_2[n, k, o] = remote(
                    second_out[n].at[k, b], second_in[n].at[k, o - 1], ssem_2.at[n, k, o - 1], rsem_2.at[n, k, o - 1], at(o)
                )
            else:
                own[n][k] = total

    def summed(n, k):
        for o in (1, 2, 3):
            got_2[n, k, o].wait_recv()
        total = own[n][k]
        for j in range(3):
            total = total + second_in[n][k, j].astype(F32)
        return total

    def hand_out(n, k, share):
        a, _, b, at = axes(n, k)
        spot = gathered[n].at[0, k, a * 4 + b]
        gathered[n][0, k, a * 4 + b] = share.astype(BF16)
        for o in (2, 1, 3):
            got_3[n, k, o] = remote(spot, spot, gsem[n][0].at[k, o - 1], gsem[n][1].at[k, o - 1], at(o))

    def activate_h(k):
        values, slope = gelu_parts(summed(0, k))
        slopes[k] = slope
        hand_out(0, k, values)

    def activate_q(k):
        hand_out(1, k, summed(1, k) * slopes[k])

    def send_4(n, k, i, first, at):
        spot = gathered[n].at[0, k, pl.ds(first, 2)]
        got_4[n, k, i] = remote(spot, spot, gsem4[n][0].at[k, i], gsem4[n][1].at[k, i], at(3 if i % 2 else 1))

    def spread(n, k):
        a, at, _, _ = axes(n, k)
        for o in (1, 2, 3):
            got_3[n, k, o].wait_recv()
        for i, first in enumerate((0, 2, 2, 0)):
            send_4(n, k, i, a * 4 + first, at)

    def relay(n, k):
        a, at, _, _ = axes(n, k)
        for way, o in ((0, 3), (1, 1)):
            got_4[n, k, way].wait_recv()
            send_4(n, k, 4 + way, (a + o) % 4 * 4 + 2 * way, at)

    def use(n, k):
        for i in range(2, 6):
            got_4[n, k, i].wait_recv()
        got_d[n, k] = remote(gathered[n].at[0, k], gathered[n].at[1, k], ssem_d.at[n, k], rsem_d.at[n, k], partner)
        weights, acc = ((dn, acc_o), (up, acc_i))[n]
        blocks = [hidden_block(n, k, p // 4, p % 4) for p in range(16)]
        left = jnp.concatenate([gathered[n][0, k, p] for p in range(16)], axis=1)
        for m in range(3):
            cols = slice(256 * m, 256 * m + 256)
            if n == 0:
                w = [jnp.concatenate([block(weights, 2 * m + u, f) for u in range(2)], axis=1) for f in blocks]
                part = dot(left, jnp.concatenate(w, axis=0))
            else:
                w = [jnp.concatenate([block(weights, 2 * m + u, f) for f in blocks], axis=1) for u in range(2)]
                part = dot_t(left, jnp.concatenate(w, axis=0))
            acc[:, cols] = part if k == 0 else acc[:, cols] + part

    def scatter(n, acc, buf, recv):
        got = []
        buf[...] = acc[...].astype(BF16)
        for o in (4, 3, 5, 2, 6, 1, 7):
            cc = (c + o) % NZ
            rows = pl.ds(pl.multiple_of(cc * ROWS, ROWS), ROWS)
            got.append(remote(buf.at[rows], recv.at[o - 1], ssem_z.at[n, o - 1], rsem_z.at[n, o - 1], at_z(o)))
        return got

    def gather_up(got, acc, recv, result):
        for copy in got:
            copy.wait_recv()
        total = acc[mine, :]
        for j in range(NZ - 1):
            total = total + recv[j].astype(F32)
        result[...] = total.astype(BF16)

    def grad_down(s, carry):
        slot = d * HALF + s
        number = slots[0, 0, slot]
        i, f = number // FB, number % FB
        k, yy, xx = f // 16, (f % 16) // 4, f % 4
        p = jnp.where(k == 1, yy * 4 + xx, xx * 4 + yy)
        hpair = jnp.concatenate([hid[0, k, p], hid[1, k, p]], axis=0)
        gpair = jnp.concatenate([gt[i, 0], gt[i, 1]], axis=0)
        part = lax.dot_general(hpair, gpair, (((0,), (0,)), ((), ())), preferred_element_type=F32)
        live = jnp.where(slot < counts[0, 0], 1.0, 0.0)
        gdn_ref[0, 0, s] = (part * live).astype(BF16)
        return carry

    def grad_up(s, carry):
        slot = d * HALF + s
        number = slots[0, 0, slot]
        i, f = number // FB, number % FB
        k, yy, xx = f // 16, (f % 16) // 4, f % 4
        p = jnp.where(k == 1, xx * 4 + yy, yy * 4 + xx)
        qpair = jnp.concatenate([pre[0, k, p], pre[1, k, p]], axis=0)
        part = dot(xt[i], qpair)
        live = jnp.where(slot < counts[0, 0], 1.0, 0.0)
        gup_ref[0, 0, s] = (part * live).astype(BF16)
        return carry

    def activate(n, k):
        (activate_h, activate_q)[n](k)

    def wait_tokens(n, k):
        for copy in (got_x, got_g)[n]:
            copy.wait_recv()
        (load_up, load_dn)[n].wait()
        if n == 0:
            for copy in tables:
                copy.wait()

    def swap_tokens(n, k):
        held = (xs, gs)[n]
        got_d["xg"[n]] = remote(held.at[0], held.at[1], ssem_d.at[2, n], rsem_d.at[2, n], partner)

    def turn(n, k):
        got_d["x"].wait_recv()
        got_d["g"].wait_recv()
        for i in range(WB):
            cols = slice(BLK * i, BLK * i + BLK)
            for half in range(2):
                xt[i, :, BLK * half : BLK * half + BLK] = xs[half, :, cols].T
                gt[i, half] = gs[half, :, cols]

    got_z = {}

    def scatter_out(n, k):
        got_z[n] = scatter(n, (acc_o, acc_i)[n], (send_o, send_i)[n], (recv_o, recv_i)[n])

    def collect(n, k):
        gather_up(got_z[n], (acc_o, acc_i)[n], (recv_o, recv_i)[n], (out_ref, gin_ref)[n])

    def gradients(n, k):
        for j in range(CHUNKS):
            got_d[n, j].wait_recv()
        for part in range(3):
            lax.fori_loop(18 * part, 18 * part + 18, (grad_down, grad_up)[n], 0, unroll=18)

    steps = dict(
        w=wait_tokens, x=swap_tokens, m=make, f=forward, s=second, a=activate, d=spread, r=relay, u=use, t=turn, z=scatter_out, c=collect, g=gradients
    )
    for step in ORDER:
        steps[step[0]](int(step[1]), int(step[2]))
    for copy in sends:
        copy.wait_send()


def write_out(*refs):
    copies = [pltpu.make_async_copy(refs[n], refs[n + 4], refs[8].at[n]) for n in range(4)]
    for copy in copies:
        copy.start()
    for copy in copies:
        copy.wait()


def on_device(inputs, up_blocks, down_blocks, slots, counts, grad_out):
    places = jnp.arange(WB * FB, dtype=jnp.int32)
    order = jnp.arange(CAP, dtype=jnp.int32)
    match = (slots[0, 0][None, :] == places[:, None]) & (order < counts[0, 0])[None, :]
    inv = jnp.min(jnp.where(match, order[None, :], CAP), axis=1)
    vmem = pl.BlockSpec(memory_space=pltpu.VMEM)
    anym = pl.BlockSpec(memory_space=pl.ANY)
    hbm = pl.BlockSpec(memory_space=pltpu.HBM)
    dma = pltpu.SemaphoreType.DMA
    scratch = [
        pltpu.SMEM((WB * FB,), jnp.int32),
        pltpu.SMEM((1, 1, CAP), jnp.int32),
        pltpu.SMEM((1, 1), jnp.int32),
        pltpu.VMEM((CAP + 1, BLK, BLK), BF16),
        pltpu.VMEM((CAP + 1, BLK, BLK), BF16),
        pltpu.VMEM((2, BLK, WB * BLK), BF16),
        pltpu.VMEM((2, BLK, WB * BLK), BF16),
        pltpu.VMEM((WB, BLK, 2 * BLK), BF16),
        pltpu.VMEM((WB, 2, BLK, BLK), BF16),
        pltpu.VMEM((CHUNKS, 4, BLK, BLK), BF16),
        pltpu.VMEM((CHUNKS, 4, BLK, BLK), BF16),
        pltpu.VMEM((CHUNKS, 2, 4, BLK, BLK), BF16),
        pltpu.VMEM((CHUNKS, 2, 4, BLK, BLK), BF16),
        pltpu.VMEM((CHUNKS, 8, BLK, BLK), F32),
        pltpu.VMEM((CHUNKS, 8, BLK, BLK), F32),
        pltpu.VMEM((CHUNKS, 2, 2, BLK, BLK), BF16),
        pltpu.VMEM((CHUNKS, 2, 2, BLK, BLK), BF16),
        pltpu.VMEM((CHUNKS, 2, 2, BLK, BLK), BF16),
        pltpu.VMEM((CHUNKS, 2, 2, BLK, BLK), BF16),
        pltpu.VMEM((CHUNKS, 3, 4, BLK, BLK), BF16),
        pltpu.VMEM((CHUNKS, 3, 4, BLK, BLK), BF16),
        pltpu.VMEM((CHUNKS, 4, BLK, BLK), BF16),
        pltpu.VMEM((CHUNKS, 4, BLK, BLK), BF16),
        pltpu.VMEM((CHUNKS, BLK, BLK), F32),
        pltpu.VMEM((CHUNKS, BLK, BLK), F32),
        pltpu.VMEM((CHUNKS, BLK, BLK), F32),
        pltpu.VMEM((CHUNKS, 3, BLK, BLK), BF16),
        pltpu.VMEM((CHUNKS, 3, BLK, BLK), BF16),
        pltpu.VMEM((2, CHUNKS, 16, BLK, BLK), BF16),
        pltpu.VMEM((2, CHUNKS, 16, BLK, BLK), BF16),
        pltpu.VMEM((BLK, WB * BLK), F32),
        pltpu.VMEM((BLK, WB * BLK), F32),
        pltpu.VMEM((BLK, WB * BLK), BF16),
        pltpu.VMEM((BLK, WB * BLK), BF16),
        pltpu.VMEM((NZ - 1, ROWS, WB * BLK), BF16),
        pltpu.VMEM((NZ - 1, ROWS, WB * BLK), BF16),
        dma((2,)),
        dma((2,)),
        dma((2, NZ)),
        dma((2, NZ)),
        dma((2, CHUNKS, 6)),
        dma((2, CHUNKS, 6)),
        dma((2, CHUNKS, 3)),
        dma((2, CHUNKS, 3)),
        dma((CHUNKS, 3)),
        dma((CHUNKS, 3)),
        dma((CHUNKS, 3)),
        dma((CHUNKS, 3)),
        dma((CHUNKS, 6)),
        dma((CHUNKS, 6)),
        dma((CHUNKS, 6)),
        dma((CHUNKS, 6)),
        dma((3, CHUNKS)),
        dma((3, CHUNKS)),
        dma((2, NZ - 1)),
        dma((2, NZ - 1)),
        dma((3,)),
    ]
    held = [pltpu.with_memory_space_constraint(a, pltpu.HBM) for a in (slots, inputs, grad_out, up_blocks, down_blocks)]
    shapes = (
        jax.ShapeDtypeStruct((ROWS, WB * BLK), BF16),
        jax.ShapeDtypeStruct((ROWS, WB * BLK), BF16),
        jax.ShapeDtypeStruct((1, 1, HALF, BLK, BLK), BF16),
        jax.ShapeDtypeStruct((1, 1, HALF, BLK, BLK), BF16),
    )
    results = pl.pallas_call(
        kernel,
        out_shape=shapes,
        in_specs=[hbm] * 7,
        out_specs=(vmem,) * 4,
        scratch_shapes=scratch,
        compiler_params=pltpu.CompilerParams(
            collective_id=0, has_side_effects=True, vmem_limit_bytes=48 * 1024 * 1024
        ),
    )(inv, held[0], counts, *held[1:])
    return pl.pallas_call(
        write_out, out_shape=shapes, in_specs=[anym] * 4, out_specs=(hbm,) * 4, scratch_shapes=[dma((4,))],
        compiler_params=pltpu.CompilerParams(vmem_limit_bytes=4 * 1024 * 1024),
    )(*results)


def solution(mesh):
    return jax.shard_map(
        on_device,
        mesh=mesh,
        in_specs=(
            P(("depth", "col"), "row"),
            P("row", "col", None, None, None),
            P("row", "col", None, None, None),
            P("row", "col", None),
            P("row", "col"),
            P(("depth", "col"), "row"),
        ),
        out_specs=(
            P(("depth", "col"), "row"),
            P(("depth", "col"), "row"),
            P("row", "col", "depth", None, None),
            P("row", "col", "depth", None, None),
        ),
        check_vma=False,
    )
```

time: 90 us -> 70.5 us (0.78)
  Pallas kernels: 81.9 us -> 68.1 us
  local copies, waits for them, and re-layouts: 5.76 us -> 0 us
    pallas_call x1, Pallas kernels: 78 us -> 66.3 us  [on_device(): pl.pallas_call(kernel, out_shape=shapes, in_specs=[hbm] * 7, out_specs=(v...]
    unnamed x14 -> x0, local copies, waits for them, and re-layouts: 5.76 us -> none
    pallas_call x1, Pallas kernels: 3.88 us -> 1.84 us  [on_device(): pl.pallas_call(write_out, out_shape=shapes, in_specs=[anym] * 4, out_spec...]
where the time goes in v3:
time: 70.5 us; the launch traced here: 70.2 us
  Pallas kernels  68.1 us (97%)
  between operations  1.29 us (2%)
  other arithmetic  0.81 us (1%)
    pallas_call x1, Pallas kernels, on_device(): pl.pallas_call(kernel, out_shape=shapes, in_specs=[hbm] * 7, out_specs=(v...  66.3 us
    pallas_call x1, Pallas kernels, on_device(): pl.pallas_call(write_out, out_shape=shapes, in_specs=[anym] * 4, out_spec...  1.84 us

profile of v3, /device:TPU:1, one launch (start us, length us, event | category | flops | bytes accessed | tf_op | source)
XLA Modules:
  0.0 70.2 jit_solution(9995022960899549116)
XLA Ops:
  1.3 0.8 %select_reduce_fusion.inv_in = s32[288]{0:T(512)S(1)} fusion(s32[108]{0:T(128)} %bitcast.3, pred[108]{0:T(512)(128)(4,1)S(1)} %iota_compare_fusion.1), kind=kLoop, calls=%fused_computation | loop fusion | flops 124128 | bytes 1692 | tf_op jit(solution)/shard_map/reduce_min | solution.py:355
  2.1 66.3 %shard_map.93 = (bf16[16,768]{1,0:T(8,128)(2,1)S(1)}, bf16[16,768]{1,0:T(8,128)(2,1)S(1)}, bf16[1,1,54,128,128]{4,3,2,1,0:T(8,128)(2,1)S(1)}, bf16[1,1,54,128,128]{4,3,2,1,0:T(8,128)(2,1)S(1)}) custom-call(s32[288]{0:T(512)S(1)} %select_reduce_fusion.inv_in, s32[1,1,108]{2,1,0:T(1,128)} %slots_in.1, s32[1,1]{1,0:T(1,128)} %copy.10.counts_in, ...), custom_call_target="tpu_custom_call" | custom-call | tf_op jit(solution)/shard_map/pallas_call | solution.py:426
  68.4 1.8 %shard_map.94 = (bf16[16,768]{1,0:T(8,128)(2,1)}, bf16[16,768]{1,0:T(8,128)(2,1)}, bf16[1,1,54,128,128]{4,3,2,1,0:T(8,128)(2,1)}, bf16[1,1,54,128,128]{4,3,2,1,0:T(8,128)(2,1)}) custom-call(bf16[16,768]{1,0:T(8,128)(2,1)S(1)} %get-tuple-element.8.refs_0_, bf16[16,768]{1,0:T(8,128)(2,1)S(1)} %get-tuple-element.9.refs_1_, ...), custom_call_target="tpu_custom_call" | custom-call | tf_op jit(solution)/shard_map/pallas_call | solution.py:436
  (1 shorter events, 0.0 us)

commit v4 on v3

--- a/solution.py
+++ b/solution.py
@@ -15,7 +15,7 @@
 ORDER = (
     "w00m00m01m02w10m10m11f00f01m12f02f10f11s00s01s02f12x00x10s10",
     "s11a00a01s12a02t00a10d00d01a11a12d02d10r00r01d11d12r02r10u00",
-    "r11u01r12u02z00u10u11u12z10g00c00g10c10",
+    "r11u01r12u02z00u10u11u12z10g00c00g10e00c10",
 )
 ORDER = [part[i : i + 3] for part in ORDER for i in range(0, len(part), 3)]
 
@@ -48,9 +48,9 @@
 
 
 def kernel(
-    inv_in, slots_in, counts_in, x_in, g_in, up_in, dn_in,
+    slots_in, counts, x_in, g_in, up_in, dn_in,
     out_ref, gin_ref, gup_ref, gdn_ref,
-    inv, slots, counts, up, dn, xs, gs, xt, gt, farp, farg, nearp, nearg, keptp, keptg, thrup, thrug, joinp, joing, r1p, r1g, s2p, s2g, ownp, owng, slopes, r2p, r2g,
+    inv, places, slots, up, dn, xs, gs, xt, gt, farp, farg, nearp, nearg, keptp, keptg, thrup, thrug, joinp, joing, r1p, r1g, s2p, s2g, ownp, owng, slopes, r2p, r2g,
     hid, pre, acc_o, acc_i, send_o, send_i, recv_o, recv_i,
     wsem, lsem, ssem_a, rsem_a, ssem_1, rsem_1, ssem_2, rsem_2, ssem_h, rsem_h, ssem_q, rsem_q, ssem_h4, rsem_h4, ssem_q4, rsem_q4,
     ssem_d, rsem_d, ssem_z, rsem_z, tsem,
@@ -83,12 +83,8 @@
     mine = pl.ds(pl.multiple_of(c * ROWS, ROWS), ROWS)
     load_x = pltpu.make_async_copy(x_in, xs.at[0, mine], lsem.at[0])
     load_g = pltpu.make_async_copy(g_in, gs.at[0, mine], lsem.at[1])
-    tables = [
-        pltpu.make_async_copy(source, held, tsem.at[n])
-        for n, (source, held) in enumerate(((inv_in, inv), (slots_in, slots), (counts_in, counts)))
-    ]
-    for copy in tables:
-        copy.start()
+    load_slots = pltpu.make_async_copy(slots_in, slots, tsem.at[0])
+    load_slots.start()
     load_x.start()
     load_g.start()
     load_up.start()
@@ -110,8 +106,21 @@
         for o in (4, 3, 5, 2, 6, 1, 7):
             got.append(remote(spot, spot, ssem_a.at[n, o], rsem_a.at[n, o], at_z(o)))
 
+    load_slots.wait()
+    tile = (8, BLK)
+    row, lane = lax.broadcasted_iota(jnp.int32, tile, 0), lax.broadcasted_iota(jnp.int32, tile, 1)
+    number = jnp.where(lane < FB, row * FB + lane, WB * FB + BLK)
+
+    def enter(slot, table):
+        wanted = jnp.where(slot < counts[0, 0], slots[0, 0, slot], -1)
+        return jnp.where(number == wanted, slot, table)
+
+    places[...] = lax.fori_loop(0, CAP, enter, jnp.full(tile, CAP, jnp.int32), unroll=12)
+    to_scalars = pltpu.make_async_copy(places, inv, tsem.at[1])
+    to_scalars.start()
+
     def block(weights, i, f):
-        return weights[inv[i * FB + f]]
+        return weights[inv[i, f]]
 
     def pair_p(fa, fb):
         acc = None
@@ -301,8 +310,7 @@
             copy.wait_recv()
         (load_up, load_dn)[n].wait()
         if n == 0:
-            for copy in tables:
-                copy.wait()
+            to_scalars.wait()
 
     def swap_tokens(n, k):
         held = (xs, gs)[n]
@@ -322,6 +330,11 @@
     def scatter_out(n, k):
         got_z[n] = scatter(n, (acc_o, acc_i)[n], (send_o, send_i)[n], (recv_o, recv_i)[n])
 
+    def finish_sends(n, k):
+        for copy in sends:
+            copy.wait_send()
+        sends.clear()
+
     def collect(n, k):
         gather_up(got_z[n], (acc_o, acc_i)[n], (recv_o, recv_i)[n], (out_ref, gin_ref)[n])
 
@@ -332,12 +345,10 @@
             lax.fori_loop(18 * part, 18 * part + 18, (grad_down, grad_up)[n], 0, unroll=18)
 
     steps = dict(
-        w=wait_tokens, x=swap_tokens, m=make, f=forward, s=second, a=activate, d=spread, r=relay, u=use, t=turn, z=scatter_out, c=collect, g=gradients
+        w=wait_tokens, x=swap_tokens, m=make, f=forward, s=second, a=activate, d=spread, r=relay, u=use, t=turn, z=scatter_out, c=collect, e=finish_sends, g=gradients
     )
     for step in ORDER:
         steps[step[0]](int(step[1]), int(step[2]))
-    for copy in sends:
-        copy.wait_send()
 
 
 def write_out(*refs):
@@ -349,18 +360,14 @@
 
 
 def on_device(inputs, up_blocks, down_blocks, slots, counts, grad_out):
-    places = jnp.arange(WB * FB, dtype=jnp.int32)
-    order = jnp.arange(CAP, dtype=jnp.int32)
-    match = (slots[0, 0][None, :] == places[:, None]) & (order < counts[0, 0])[None, :]
-    inv = jnp.min(jnp.where(match, order[None, :], CAP), axis=1)
     vmem = pl.BlockSpec(memory_space=pltpu.VMEM)
     anym = pl.BlockSpec(memory_space=pl.ANY)
     hbm = pl.BlockSpec(memory_space=pltpu.HBM)
     dma = pltpu.SemaphoreType.DMA
     scratch = [
-        pltpu.SMEM((WB * FB,), jnp.int32),
+        pltpu.SMEM((8, BLK), jnp.int32),
+        pltpu.VMEM((8, BLK), jnp.int32),
         pltpu.SMEM((1, 1, CAP), jnp.int32),
-        pltpu.SMEM((1, 1), jnp.int32),
         pltpu.VMEM((CAP + 1, BLK, BLK), BF16),
         pltpu.VMEM((CAP + 1, BLK, BLK), BF16),
         pltpu.VMEM((2, BLK, WB * BLK), BF16),
@@ -414,7 +421,7 @@
         dma((3, CHUNKS)),
         dma((2, NZ - 1)),
         dma((2, NZ - 1)),
-        dma((3,)),
+        dma((2,)),
     ]
     held = [pltpu.with_memory_space_constraint(a, pltpu.HBM) for a in (slots, inputs, grad_out, up_blocks, down_blocks)]
     shapes = (
@@ -426,13 +433,13 @@
     results = pl.pallas_call(
         kernel,
         out_shape=shapes,
-        in_specs=[hbm] * 7,
+        in_specs=[hbm, pl.BlockSpec(memory_space=pltpu.SMEM)] + [hbm] * 4,
         out_specs=(vmem,) * 4,
         scratch_shapes=scratch,
         compiler_params=pltpu.CompilerParams(
             collective_id=0, has_side_effects=True, vmem_limit_bytes=48 * 1024 * 1024
         ),
-    )(inv, held[0], counts, *held[1:])
+    )(held[0], counts, *held[1:])
     return pl.pallas_call(
         write_out, out_shape=shapes, in_specs=[anym] * 4, out_specs=(hbm,) * 4, scratch_shapes=[dma((4,))],
         compiler_params=pltpu.CompilerParams(vmem_limit_bytes=4 * 1024 * 1024),

time: 70.5 us -> 69.5 us (0.986)
  other arithmetic: 0.81 us -> 0 us
    reduce_min x1 -> x0, other arithmetic: 0.81 us -> none  [on_device(): inv = jnp.min(jnp.where(match, order[None, :], CAP), axis=1)]
where the time goes in v4:
time: 69.5 us; the launch traced here: 69.3 us
  Pallas kernels  68 us (98%)
  between operations  1.29 us (2%)
    pallas_call x1, Pallas kernels, on_device(): pl.pallas_call(kernel, out_shape=shapes, in_specs=[hbm, pl.BlockSpec(memo...  66.1 us
    pallas_call x1, Pallas kernels, on_device(): pl.pallas_call(write_out, out_shape=shapes, in_specs=[anym] * 4, out_spec...  1.84 us

profile of v4, /device:TPU:1, one launch (start us, length us, event | category | flops | bytes accessed | tf_op | source)
XLA Modules:
  0.0 69.3 jit_solution(11562746538959260448)
XLA Ops:
  1.3 66.1 %shard_map.93 = (bf16[16,768]{1,0:T(8,128)(2,1)S(1)}, bf16[16,768]{1,0:T(8,128)(2,1)S(1)}, bf16[1,1,54,128,128]{4,3,2,1,0:T(8,128)(2,1)S(1)}, bf16[1,1,54,128,128]{4,3,2,1,0:T(8,128)(2,1)S(1)}) custom-call(s32[1,1,108]{2,1,0:T(1,128)} %slots_in.1, s32[1,1]{1,0:T(1,128)S(6)} %copy.10.counts, bf16[16,768]{1,0:T(8,128)(2,1)} %x_in.1, bf16[16,768]{1,0:T(8,128)(2,1)} %g_in.1, ...), custom_call_target="tpu_custom_call" | custom-call | tf_op jit(solution)/shard_map/pallas_call | solution.py:433
  67.4 1.8 %shard_map.94 = (bf16[16,768]{1,0:T(8,128)(2,1)}, bf16[16,768]{1,0:T(8,128)(2,1)}, bf16[1,1,54,128,128]{4,3,2,1,0:T(8,128)(2,1)}, bf16[1,1,54,128,128]{4,3,2,1,0:T(8,128)(2,1)}) custom-call(bf16[16,768]{1,0:T(8,128)(2,1)S(1)} %get-tuple-element.8.refs_0_, bf16[16,768]{1,0:T(8,128)(2,1)S(1)} %get-tuple-element.9.refs_1_, ...), custom_call_target="tpu_custom_call" | custom-call | tf_op jit(solution)/shard_map/pallas_call | solution.py:443

commit v5 on v4

--- a/solution.py
+++ b/solution.py
@@ -15,8 +15,9 @@
 ORDER = (
     "w00m00m01m02w10m10m11f00f01m12f02f10f11s00s01s02f12x00x10s10",
     "s11a00a01s12a02t00a10d00d01a11a12d02d10r00r01d11d12r02r10u00",
-    "r11u01r12u02z00u10u11u12z10g00c00g10e00c10",
+    "r11u01r12u02z00u10u11v12u12z10g00c00g10e00c10",
 )
+LAST = (1, 2)
 ORDER = [part[i : i + 3] for part in ORDER for i in range(0, len(part), 3)]
 
 root_coeff = 0.7978845608
@@ -243,13 +244,10 @@
             got_4[n, k, way].wait_recv()
             send_4(n, k, 4 + way, (a + o) % 4 * 4 + 2 * way, at)
 
-    def use(n, k):
-        for i in range(2, 6):
-            got_4[n, k, i].wait_recv()
-        got_d[n, k] = remote(gathered[n].at[0, k], gathered[n].at[1, k], ssem_d.at[n, k], rsem_d.at[n, k], partner)
+    def multiply(n, k, first, places):
         weights, acc = ((dn, acc_o), (up, acc_i))[n]
-        blocks = [hidden_block(n, k, p // 4, p % 4) for p in range(16)]
-        left = jnp.concatenate([gathered[n][0, k, p] for p in range(16)], axis=1)
+        blocks = [hidden_block(n, k, a, b) for a, b in places]
+        left = jnp.concatenate([gathered[n][0, k, a * 4 + b] for a, b in places], axis=1)
         for m in range(3):
             cols = slice(256 * m, 256 * m + 256)
             if n == 0:
@@ -258,7 +256,26 @@
             else:
                 w = [jnp.concatenate([block(weights, 2 * m + u, f) for f in blocks], axis=1) for u in range(2)]
                 part = dot_t(left, jnp.concatenate(w, axis=0))
-            acc[:, cols] = part if k == 0 else acc[:, cols] + part
+            acc[:, cols] = part if first else acc[:, cols] + part
+
+    def group(n, k, *offsets):
+        here = axes(n, k)[0]
+        return [((here + o) % 4, b) for o in offsets for b in range(4)]
+
+    def use_near(n, k):
+        for i in (2, 3):
+            got_4[n, k, i].wait_recv()
+        multiply(n, k, k == 0, group(n, k, 0, 1, 3))
+
+    def use(n, k):
+        split = (n, k) == LAST
+        for i in (4, 5) if split else range(2, 6):
+            got_4[n, k, i].wait_recv()
+        got_d[n, k] = remote(gathered[n].at[0, k], gathered[n].at[1, k], ssem_d.at[n, k], rsem_d.at[n, k], partner)
+        if split:
+            multiply(n, k, False, group(n, k, 2))
+        else:
+            multiply(n, k, k == 0, [(p // 4, p % 4) for p in range(16)])
 
     def scatter(n, acc, buf, recv):
         got = []
@@ -345,7 +362,7 @@
             lax.fori_loop(18 * part, 18 * part + 18, (grad_down, grad_up)[n], 0, unroll=18)
 
     steps = dict(
-        w=wait_tokens, x=swap_tokens, m=make, f=forward, s=second, a=activate, d=spread, r=relay, u=use, t=turn, z=scatter_out, c=collect, e=finish_sends, g=gradients
+        w=wait_tokens, x=swap_tokens, m=make, f=forward, s=second, a=activate, d=spread, r=relay, u=use, v=use_near, t=turn, z=scatter_out, c=collect, e=finish_sends, g=gradients
     )
     for step in ORDER:
         steps[step[0]](int(step[1]), int(step[2]))

time: 69.5 us -> 69.5 us (level)
  no operation moved by 1% of the time
where the time goes in v5:
time: 69.5 us; the launch traced here: 69.3 us
  Pallas kernels  68 us (98%)
  between operations  1.29 us (2%)
    pallas_call x1, Pallas kernels, on_device(): pl.pallas_call(kernel, out_shape=shapes, in_specs=[hbm, pl.BlockSpec(memo...  66.1 us
    pallas_call x1, Pallas kernels, on_device(): pl.pallas_call(write_out, out_shape=shapes, in_specs=[anym] * 4, out_spec...  1.84 us

profile of v5, /device:TPU:1, one launch (start us, length us, event | category | flops | bytes accessed | tf_op | source)
XLA Modules:
  0.0 69.3 jit_solution(5332991668054816820)
XLA Ops:
  1.3 66.1 %shard_map.93 = (bf16[16,768]{1,0:T(8,128)(2,1)S(1)}, bf16[16,768]{1,0:T(8,128)(2,1)S(1)}, bf16[1,1,54,128,128]{4,3,2,1,0:T(8,128)(2,1)S(1)}, bf16[1,1,54,128,128]{4,3,2,1,0:T(8,128)(2,1)S(1)}) custom-call(s32[1,1,108]{2,1,0:T(1,128)} %slots_in.1, s32[1,1]{1,0:T(1,128)S(6)} %copy.10.counts, bf16[16,768]{1,0:T(8,128)(2,1)} %x_in.1, bf16[16,768]{1,0:T(8,128)(2,1)} %g_in.1, ...), custom_call_target="tpu_custom_call" | custom-call | tf_op jit(solution)/shard_map/pallas_call | solution.py:450
  67.4 1.8 %shard_map.94 = (bf16[16,768]{1,0:T(8,128)(2,1)}, bf16[16,768]{1,0:T(8,128)(2,1)}, bf16[1,1,54,128,128]{4,3,2,1,0:T(8,128)(2,1)}, bf16[1,1,54,128,128]{4,3,2,1,0:T(8,128)(2,1)}) custom-call(bf16[16,768]{1,0:T(8,128)(2,1)S(1)} %get-tuple-element.8.refs_0_, bf16[16,768]{1,0:T(8,128)(2,1)S(1)} %get-tuple-element.9.refs_1_, ...), custom_call_target="tpu_custom_call" | custom-call | tf_op jit(solution)/shard_map/pallas_call | solution.py:460
